TPU v7x, 32 devices: a whole 2x2x4 slice. The times are simulated.
32 devices in a mesh: groups: 2 (over x), sub: 16 (over z, y, core).
Axes of the slice: x: 2, y: 2, z: 4, core: 2. Of those that a mesh axis runs over, the one named last changes fastest.
Arguments:
- heat_source: float32 [8192, 512], P(('groups', 'sub')), parts along dimension 0, may hold values from -6 to 6
- start_temp: float32 [8192, 512], P(('groups', 'sub')), parts along dimension 0, may hold values from -6 to 6
- conduct_shift: float32 [8192, 512], P(('groups', 'sub')), parts along dimension 0, may hold values from 0.02 to 0.5
- slave_face: int32 [32768], P(('groups', 'sub')), parts along dimension 0, may hold values from 0 to 8191, as said below
- master_face: int32 [32768], P(('groups', 'sub')), parts along dimension 0, may hold values from 0 to 8191, as said below
- d_weight: float32 [32768], P(('groups', 'sub')), parts along dimension 0, may hold values from 0.5 to 1.5
- m_weight: float32 [32768], P(('groups', 'sub')), parts along dimension 0, may hold values from 0.3 to 1.2
- gap_cond: float32 [32768], P(('groups', 'sub')), parts along dimension 0, may hold values from 0.5 to 4
- active: int32 [32768], P(('groups', 'sub')), parts along dimension 0, may hold values 0 or 1
Outputs:
- temperature: float32 [8192, 512], P(('groups', 'sub')), parts along dimension 0
- final_residual: float32 [8192, 512], P(('groups', 'sub')), parts along dimension 0
There are 2 independent parts, one for each index of `groups`. A program takes and returns all parts, laid end to end along the dimension named above; each array names one. Nothing has to cross between parts.
Inputs may be any that keep to these rules, and one draw needn't show every extreme that they name: `slave_face`: the face node k * 512 + c belongs to subdomain k. The 1024 pairs listed on one subdomain name slave nodes of exactly 8 subdomains, 128 pairs on each. `master_face`: the 1024 pairs listed on one subdomain name master nodes of exactly 8 subdomains, 128 pairs on each.
All inputs are finite; a program needn't handle non-finite values. No bound on the sum of `active` on one device may be relied on, other than what follows from the above.
Results may differ from a plain program's by a relative error of at most 0.00027.
Values sent between devices are 32-bit elements; how exact they have to be, the bound alone decides.
A program may use at most 64 MiB of HBM per device.

v0:
```python
import jax
import jax.numpy as jnp
from jax import lax
from jax.sharding import PartitionSpec as P

NEWTON = 2
CG_ITERS = 2


def with_halo(block, sides, width):
    for axis, dim in sides:
        count = lax.axis_size(axis)
        forward = [(i, i + 1) for i in range(count - 1)]
        backward = [(target, source) for source, target in forward]
        low = lax.ppermute(
            lax.slice_in_dim(block, block.shape[dim] - width, None, axis=dim), axis, forward
        )
        high = lax.ppermute(lax.slice_in_dim(block, 0, width, axis=dim), axis, backward)
        block = jnp.concatenate([low, block, high], axis=dim)
    return block


def squares(resvec):
    return lax.psum(jnp.sum(resvec * resvec), "sub")


def return_faces(values):
    return lax.psum_scatter(values, "sub", scatter_dimension=0, tiled=True)


def on_device(
    heat_source,
    start_temp,
    conduct_shift,
    slave_face,
    master_face,
    d_weight,
    m_weight,
    gap_cond,
    active,
):
    width = heat_source.shape[1]
    owners_count = lax.axis_size("sub")
    faces_total = width * owners_count
    live = active.astype(jnp.float32) * gap_cond

    def contact_terms(field_row, contribute):
        faces = lax.all_gather(field_row, "sub", axis=0, tiled=True)
        gap = d_weight * faces[slave_face] - m_weight * faces[master_face]
        weights, extra = contribute(gap)
        total = jnp.zeros((faces_total,), jnp.float32)
        total = total.at[slave_face].add(d_weight * weights)
        total = total.at[master_face].add(-m_weight * weights)
        return (return_faces(total), extra)

    def operate(field, contribute):
        padded = with_halo(field, (("sub", 0),), 1)
        row_add, extra = contact_terms(field[0], contribute)
        padded = jnp.pad(padded, ((0, 0), (1, 1)))
        beside = padded[2:, 1:-1] + padded[:-2, 1:-1] + padded[1:-1, 2:] + padded[1:-1, :-2]
        result = (4.0 + conduct_shift) * field - beside
        result = result.at[0].add(row_add)
        return (result, extra)

    def nonlinear(temp):

        def nonlinear_contact(gap):
            flux = live * (2.0 * gap - jnp.arctan(gap))
            slope = live * (2.0 - 1.0 / (1.0 + gap * gap))
            return (flux, slope)

        result, slope = operate(temp, nonlinear_contact)
        return (result - heat_source, slope)

    temp = start_temp
    for newton in range(NEWTON):
        resid, slope = nonlinear(temp)
        resvec = -resid
        update = jnp.zeros_like(temp)
        direction = resvec
        norm_now = squares(resvec)
        for step in range(CG_ITERS):

            def jacobian_contact(gap):
                return (slope * gap, slope)

            jacobian_result, jacobian_unused = operate(direction, jacobian_contact)
            alpha = norm_now / lax.psum(jnp.sum(direction * jacobian_result), "sub")
            update = update + alpha * direction
            resvec = resvec - alpha * jacobian_result
            norm_next = squares(resvec)
            direction = resvec + norm_next / norm_now * direction
            norm_now = norm_next
        temp = temp + update
    final_residual, unused = nonlinear(temp)
    return (temp, final_residual)


def solution(mesh):
    in_specs = (
        P(("groups", "sub"), None),
        P(("groups", "sub"), None),
        P(("groups", "sub"), None),
        P(("groups", "sub")),
        P(("groups", "sub")),
        P(("groups", "sub")),
        P(("groups", "sub")),
        P(("groups", "sub")),
        P(("groups", "sub")),
    )
    out_specs = (P(("groups", "sub"), None), P(("groups", "sub"), None))
    return jax.shard_map(
        on_device, mesh=mesh, in_specs=in_specs, out_specs=out_specs, check_vma=False
    )
```

profile of v0, /device:TPU:0, one launch (start us, length us, event | category | flops | bytes accessed | tf_op | source)
XLA Modules:
  0.0 949.7 jit_solution(15990991822109688646)
XLA Ops:
  5.0 25.1 %all-gather = f32[1,8192]{1,0:T(1,128)S(1)} all-gather(f32[1,512]{1,0:T(1,128)S(1)} %get-tuple-element.120), channel_id=2, replica_groups=mesh['groups'=2,'sub'=16] {'sub'}, dimensions={1}, use_global_device_ids=true | all-gather | bytes 34816 | tf_op jit(solution)/shard_map/all_gather | solution.py:48
  30.8 6.1 gather_fusion.1
  37.0 6.2 gather_fusion
  55.4 57.8 %all-reduce.7 = f32[8192]{0:T(1024)S(1)} all-reduce(f32[8192]{0:T(1024)S(1)} %scatter_fusion), channel_id=9, replica_groups=mesh['groups'=2,'sub'=16] {'sub'}, use_global_device_ids=true, to_apply=%region_2.0.clone | all-reduce | flops 8192 | bytes 65536
  122.5 18.3 %all-gather.1 = f32[1,8192]{1,0:T(1,128)S(1)} all-gather(f32[1,512]{1,0:T(1,128)S(1)} %get-tuple-element.118), channel_id=3, replica_groups=mesh['groups'=2,'sub'=16] {'sub'}, dimensions={1}, use_global_device_ids=true | all-gather | bytes 34816 | tf_op jit(solution)/shard_map/all_gather | solution.py:48
  140.8 6.1 gather_fusion.3
  146.9 6.2 gather_fusion.2
  167.4 58.2 %all-reduce.8 = f32[8192]{0:T(1024)S(1)} all-reduce(f32[8192]{0:T(1024)S(1)} %scatter_fusion.1), channel_id=10, replica_groups=mesh['groups'=2,'sub'=16] {'sub'}, use_global_device_ids=true, to_apply=%region_7.8.clone | all-reduce | flops 8192 | bytes 65536
  227.1 30.1 %all-reduce.15 = (f32[]{:T(128)}, f32[]{:T(128)}) all-reduce(f32[]{:T(128)} %get-tuple-element.105, f32[]{:T(128)} %multiply_reduce_fusion.6), channel_id=1, replica_groups=mesh['groups'=2,'sub'=16] {'sub'}, use_global_device_ids=true, to_apply=%region_4.5 | all-reduce | flops 2 | bytes 16 | tf_op jit(solution)/shard_map/psum | solution.py:24
  259.3 30.1 %psum.58 = f32[]{:T(128)} all-reduce(f32[]{:T(128)} %multiply_reduce_fusion.5), channel_id=1, replica_groups=mesh['groups'=2,'sub'=16] {'sub'}, use_global_device_ids=true, to_apply=%region_11.12 | all-reduce | flops 1 | bytes 8 | tf_op jit(solution)/shard_map/psum | solution.py:24
  292.2 19.3 %all-gather.2 = f32[1,8192]{1,0:T(1,128)S(1)} all-gather(f32[1,512]{1,0:T(1,128)S(1)} %get-tuple-element.116), channel_id=4, replica_groups=mesh['groups'=2,'sub'=16] {'sub'}, dimensions={1}, use_global_device_ids=true | all-gather | bytes 34816 | tf_op jit(solution)/shard_map/all_gather | solution.py:48
  311.5 6.1 gather_fusion.5
  317.6 6.2 gather_fusion.4
  338.3 57.6 %all-reduce.9 = f32[8192]{0:T(1024)S(1)} all-reduce(f32[8192]{0:T(1024)S(1)} %scatter_fusion.2), channel_id=11, replica_groups=mesh['groups'=2,'sub'=16] {'sub'}, use_global_device_ids=true, to_apply=%region_14.15.clone | all-reduce | flops 8192 | bytes 65536
  397.4 30.1 %psum.59 = f32[]{:T(128)} all-reduce(f32[]{:T(128)} %multiply_reduce_fusion.4), channel_id=1, replica_groups=mesh['groups'=2,'sub'=16] {'sub'}, use_global_device_ids=true, to_apply=%region_16.17 | all-reduce | flops 1 | bytes 8 | tf_op jit(solution)/shard_map/psum | solution.py:88
  430.4 19.3 %all-gather.3 = f32[1,8192]{1,0:T(1,128)S(1)} all-gather(f32[1,512]{1,0:T(1,128)S(1)} %get-tuple-element.114), channel_id=5, replica_groups=mesh['groups'=2,'sub'=16] {'sub'}, dimensions={1}, use_global_device_ids=true | all-gather | bytes 34816 | tf_op jit(solution)/shard_map/all_gather | solution.py:48
  455.8 6.2 gather_fusion.6
  476.3 57.6 %all-reduce.10 = f32[8192]{0:T(1024)S(1)} all-reduce(f32[8192]{0:T(1024)S(1)} %scatter_fusion.3), channel_id=12, replica_groups=mesh['groups'=2,'sub'=16] {'sub'}, use_global_device_ids=true, to_apply=%region_19.20.clone | all-reduce | flops 8192 | bytes 65536
  536.8 18.3 %all-gather.4 = f32[1,8192]{1,0:T(1,128)S(1)} all-gather(f32[1,512]{1,0:T(1,128)S(1)} %get-tuple-element.112), channel_id=6, replica_groups=mesh['groups'=2,'sub'=16] {'sub'}, dimensions={1}, use_global_device_ids=true | all-gather | bytes 34816 | tf_op jit(solution)/shard_map/all_gather | solution.py:48
  555.1 6.1 gather_fusion.9
  561.2 6.2 gather_fusion.8
  581.8 58.2 %all-reduce.11 = f32[8192]{0:T(1024)S(1)} all-reduce(f32[8192]{0:T(1024)S(1)} %scatter_fusion.4), channel_id=13, replica_groups=mesh['groups'=2,'sub'=16] {'sub'}, use_global_device_ids=true, to_apply=%region_24.25.clone | all-reduce | flops 8192 | bytes 65536
  641.4 30.1 %all-reduce.14 = (f32[]{:T(128)}, f32[]{:T(128)}) all-reduce(f32[]{:T(128)} %get-tuple-element.103, f32[]{:T(128)} %multiply_reduce_fusion.2), channel_id=1, replica_groups=mesh['groups'=2,'sub'=16] {'sub'}, use_global_device_ids=true, to_apply=%region_21.22 | all-reduce | flops 2 | bytes 16 | tf_op jit(solution)/shard_map/psum | solution.py:24
  673.7 30.1 %psum.62 = f32[]{:T(128)} all-reduce(f32[]{:T(128)} %multiply_reduce_fusion.1), channel_id=1, replica_groups=mesh['groups'=2,'sub'=16] {'sub'}, use_global_device_ids=true, to_apply=%region_28.29 | all-reduce | flops 1 | bytes 8 | tf_op jit(solution)/shard_map/psum | solution.py:24
  706.5 19.3 %all-gather.5 = f32[1,8192]{1,0:T(1,128)S(1)} all-gather(f32[1,512]{1,0:T(1,128)S(1)} %get-tuple-element.110), channel_id=7, replica_groups=mesh['groups'=2,'sub'=16] {'sub'}, dimensions={1}, use_global_device_ids=true | all-gather | bytes 34816 | tf_op jit(solution)/shard_map/all_gather | solution.py:48
  725.8 6.1 gather_fusion.11
  732.0 6.2 gather_fusion.10
  752.5 57.6 %all-reduce.12 = f32[8192]{0:T(1024)S(1)} all-reduce(f32[8192]{0:T(1024)S(1)} %scatter_fusion.5), channel_id=14, replica_groups=mesh['groups'=2,'sub'=16] {'sub'}, use_global_device_ids=true, to_apply=%region_31.32.clone | all-reduce | flops 8192 | bytes 65536
  811.6 30.1 %psum.63 = f32[]{:T(128)} all-reduce(f32[]{:T(128)} %multiply_reduce_fusion), channel_id=1, replica_groups=mesh['groups'=2,'sub'=16] {'sub'}, use_global_device_ids=true, to_apply=%region_33.34 | all-reduce | flops 1 | bytes 8 | tf_op jit(solution)/shard_map/psum | solution.py:88
  844.5 19.3 %all-gather.6 = f32[1,8192]{1,0:T(1,128)S(1)} all-gather(f32[1,512]{1,0:T(1,128)S(1)} %get-tuple-element.108), channel_id=8, replica_groups=mesh['groups'=2,'sub'=16] {'sub'}, dimensions={1}, use_global_device_ids=true | all-gather | bytes 34816 | tf_op jit(solution)/shard_map/all_gather | solution.py:48
  870.0 6.2 gather_fusion.12
  890.5 57.6 %all-reduce.13 = f32[8192]{0:T(1024)S(1)} all-reduce(f32[8192]{0:T(1024)S(1)} %scatter_fusion.6), channel_id=15, replica_groups=mesh['groups'=2,'sub'=16] {'sub'}, use_global_device_ids=true, to_apply=%region_36.37.clone | all-reduce | flops 8192 | bytes 65536
  (137 shorter events, 141.7 us)
Async XLA Ops:
  1.4 113.8 %collective-permute-start.1 = (f32[1,512]{1,0:T(1,128)S(1)}, f32[1,512]{1,0:T(1,128)S(1)}, u32[]{:S(2)}, u32[]{:S(2)}) collective-permute-start(f32[1,512]{1,0:T(1,128)S(1)} %get-tuple-element.119), channel_id=1, source_target_pairs={{0,1},{1,2},{2,3},{3,4},{4,5},{5,6},{6,7},{7,8},{8,9},{9,10},{10,1... | collective-permute-start | bytes 6152 | tf_op jit(solution)/shard_map/ppermute | solution.py:15
  3.7 26.4 %copy-start.6 = (s32[1024]{0:T(1024)S(1)}, s32[1024]{0:T(1024)}, u32[]{:S(2)}) copy-start(s32[1024]{0:T(1024)} %param.26) | copy-start | bytes 12292
  3.7 111.4 %collective-permute-start = (f32[1,512]{1,0:T(1,128)S(1)}, f32[1,512]{1,0:T(1,128)S(1)}, u32[]{:S(2)}, u32[]{:S(2)}) collective-permute-start(f32[1,512]{1,0:T(1,128)S(1)} %get-tuple-element.120), channel_id=1, source_target_pairs={{1,0},{2,1},{3,2},{4,3},{5,4},{6,5},{7,6},{8,7},{9,8},{10,9},{11,1... | collective-permute-start | bytes 6152 | tf_op jit(solution)/shard_map/ppermute | solution.py:18
  30.1 0.7 copy-start.7
  37.0 6.2 copy-start.4
  37.0 6.2 copy-start.5
  37.0 6.2 copy-start.8
  37.0 6.2 copy-start.9
  49.3 65.9 %copy-start.1 = (f32[256,512]{1,0:T(8,128)S(1)}, f32[256,512]{1,0:T(8,128)}, u32[]{:S(2)}) copy-start(f32[256,512]{1,0:T(8,128)} %param.24) | copy-start | bytes 1572868
  113.2 0.7 copy-start.10
  115.2 1.0 copy-start
  116.2 3.2 copy-start.3
  121.2 104.5 %collective-permute-start.2 = (f32[1,512]{1,0:T(1,128)S(1)}, f32[1,512]{1,0:T(1,128)S(1)}, u32[]{:S(2)}, u32[]{:S(2)}) collective-permute-start(f32[1,512]{1,0:T(1,128)S(1)} %get-tuple-element.118), channel_id=1, source_target_pairs={{1,0},{2,1},{3,2},{4,3},{5,4},{6,5},{7,6},{8,7},{9,8},{10,9},{11,1... | collective-permute-start | bytes 6152 | tf_op jit(solution)/shard_map/ppermute | solution.py:18
  153.1 72.6 %collective-permute-start.3 = (f32[1,512]{1,0:T(1,128)S(1)}, f32[1,512]{1,0:T(1,128)S(1)}, u32[]{:S(2)}, u32[]{:S(2)}) collective-permute-start(f32[1,512]{1,0:T(1,128)S(1)} %get-tuple-element.117), channel_id=1, source_target_pairs={{0,1},{1,2},{2,3},{3,4},{4,5},{5,6},{6,7},{7,8},{8,9},{9,10},{10,1... | collective-permute-start | bytes 6152 | tf_op jit(solution)/shard_map/ppermute | solution.py:15
  290.9 105.1 %collective-permute-start.4 = (f32[1,512]{1,0:T(1,128)S(1)}, f32[1,512]{1,0:T(1,128)S(1)}, u32[]{:S(2)}, u32[]{:S(2)}) collective-permute-start(f32[1,512]{1,0:T(1,128)S(1)} %get-tuple-element.116), channel_id=1, source_target_pairs={{1,0},{2,1},{3,2},{4,3},{5,4},{6,5},{7,6},{8,7},{9,8},{10,9},{11,1... | collective-permute-start | bytes 6152 | tf_op jit(solution)/shard_map/ppermute | solution.py:18
  323.8 72.2 %collective-permute-start.5 = (f32[1,512]{1,0:T(1,128)S(1)}, f32[1,512]{1,0:T(1,128)S(1)}, u32[]{:S(2)}, u32[]{:S(2)}) collective-permute-start(f32[1,512]{1,0:T(1,128)S(1)} %get-tuple-element.115), channel_id=1, source_target_pairs={{0,1},{1,2},{2,3},{3,4},{4,5},{5,6},{6,7},{7,8},{8,9},{9,10},{10,1... | collective-permute-start | bytes 6152 | tf_op jit(solution)/shard_map/ppermute | solution.py:15
  429.1 105.0 %collective-permute-start.6 = (f32[1,512]{1,0:T(1,128)S(1)}, f32[1,512]{1,0:T(1,128)S(1)}, u32[]{:S(2)}, u32[]{:S(2)}) collective-permute-start(f32[1,512]{1,0:T(1,128)S(1)} %get-tuple-element.114), channel_id=1, source_target_pairs={{1,0},{2,1},{3,2},{4,3},{5,4},{6,5},{7,6},{8,7},{9,8},{10,9},{11,1... | collective-permute-start | bytes 6152 | tf_op jit(solution)/shard_map/ppermute | solution.py:18
  461.9 72.1 %collective-permute-start.7 = (f32[1,512]{1,0:T(1,128)S(1)}, f32[1,512]{1,0:T(1,128)S(1)}, u32[]{:S(2)}, u32[]{:S(2)}) collective-permute-start(f32[1,512]{1,0:T(1,128)S(1)} %get-tuple-element.113), channel_id=1, source_target_pairs={{0,1},{1,2},{2,3},{3,4},{4,5},{5,6},{6,7},{7,8},{8,9},{9,10},{10,1... | collective-permute-start | bytes 6152 | tf_op jit(solution)/shard_map/ppermute | solution.py:15
  535.5 104.5 %collective-permute-start.8 = (f32[1,512]{1,0:T(1,128)S(1)}, f32[1,512]{1,0:T(1,128)S(1)}, u32[]{:S(2)}, u32[]{:S(2)}) collective-permute-start(f32[1,512]{1,0:T(1,128)S(1)} %get-tuple-element.112), channel_id=1, source_target_pairs={{1,0},{2,1},{3,2},{4,3},{5,4},{6,5},{7,6},{8,7},{9,8},{10,9},{11,1... | collective-permute-start | bytes 6152 | tf_op jit(solution)/shard_map/ppermute | solution.py:18
  567.4 72.6 %collective-permute-start.9 = (f32[1,512]{1,0:T(1,128)S(1)}, f32[1,512]{1,0:T(1,128)S(1)}, u32[]{:S(2)}, u32[]{:S(2)}) collective-permute-start(f32[1,512]{1,0:T(1,128)S(1)} %get-tuple-element.111), channel_id=1, source_target_pairs={{0,1},{1,2},{2,3},{3,4},{4,5},{5,6},{6,7},{7,8},{8,9},{9,10},{10,1... | collective-permute-start | bytes 6152 | tf_op jit(solution)/shard_map/ppermute | solution.py:15
  705.2 105.0 %collective-permute-start.10 = (f32[1,512]{1,0:T(1,128)S(1)}, f32[1,512]{1,0:T(1,128)S(1)}, u32[]{:S(2)}, u32[]{:S(2)}) collective-permute-start(f32[1,512]{1,0:T(1,128)S(1)} %get-tuple-element.110), channel_id=1, source_target_pairs={{1,0},{2,1},{3,2},{4,3},{5,4},{6,5},{7,6},{8,7},{9,8},{10,9},{11,1... | collective-permute-start | bytes 6152 | tf_op jit(solution)/shard_map/ppermute | solution.py:18
  738.1 72.1 %collective-permute-start.11 = (f32[1,512]{1,0:T(1,128)S(1)}, f32[1,512]{1,0:T(1,128)S(1)}, u32[]{:S(2)}, u32[]{:S(2)}) collective-permute-start(f32[1,512]{1,0:T(1,128)S(1)} %get-tuple-element.109), channel_id=1, source_target_pairs={{0,1},{1,2},{2,3},{3,4},{4,5},{5,6},{6,7},{7,8},{8,9},{9,10},{10,1... | collective-permute-start | bytes 6152 | tf_op jit(solution)/shard_map/ppermute | solution.py:15
  843.2 105.3 %copy-start.2 = (f32[256,512]{1,0:T(8,128)}, f32[256,512]{1,0:T(8,128)S(1)}, u32[]{:S(2)}) copy-start(f32[256,512]{1,0:T(8,128)S(1)} %add_add_fusion) | copy-start | bytes 1572868
  843.2 105.0 %collective-permute-start.12 = (f32[1,512]{1,0:T(1,128)S(1)}, f32[1,512]{1,0:T(1,128)S(1)}, u32[]{:S(2)}, u32[]{:S(2)}) collective-permute-start(f32[1,512]{1,0:T(1,128)S(1)} %get-tuple-element.108), channel_id=1, source_target_pairs={{1,0},{2,1},{3,2},{4,3},{5,4},{6,5},{7,6},{8,7},{9,8},{10,9},{11,1... | collective-permute-start | bytes 6152 | tf_op jit(solution)/shard_map/ppermute | solution.py:18
  876.1 72.1 %collective-permute-start.13 = (f32[1,512]{1,0:T(1,128)S(1)}, f32[1,512]{1,0:T(1,128)S(1)}, u32[]{:S(2)}, u32[]{:S(2)}) collective-permute-start(f32[1,512]{1,0:T(1,128)S(1)} %get-tuple-element.107), channel_id=1, source_target_pairs={{0,1},{1,2},{2,3},{3,4},{4,5},{5,6},{6,7},{7,8},{8,9},{9,10},{10,1... | collective-permute-start | bytes 6152 | tf_op jit(solution)/shard_map/ppermute | solution.py:15
where the time goes:
time: 951 us; the launch traced here: 950 us
  blocking collectives  724 us (76%)
  other arithmetic  98.7 us (10%)
  local copies, waits for them, and re-layouts  91.8 us (10%)
  starting transfers between devices  25 us (3%)
  between operations  10 us (1%)
    unnamed x7, blocking collectives  405 us
    all_gather x7, blocking collectives, contact_terms(): faces = lax.all_gather(field_row, 'sub', axis=0, tiled=True)  139 us
    psum x4, blocking collectives, squares(): return lax.psum(jnp.sum(resvec * resvec), 'sub')  120 us
    gather x14, local copies, waits for them, and re-layouts, contact_terms(): gap = d_weight * faces[slave_face] - m_weight * faces[master_face]  86.1 us
    psum x2, blocking collectives, on_device(): alpha = norm_now / lax.psum(jnp.sum(direction * jacobian_result), 'sub')  60.2 us
    scatter-add x7, other arithmetic, contact_terms(): total = total.at[master_face].add(-m_weight * weights)  42.8 us
    scatter-add x7, other arithmetic, contact_terms(): total = total.at[slave_face].add(d_weight * weights)  41.6 us
  transfers between devices with their start and end apart: 14, of which 0 were waited for; matrix products, arithmetic and copies ran while one was open for 18% of the time, Pallas kernels for 0%

commit v1 on v0

v1 whole, which is shorter than its diff:
```python
import functools

import jax
import jax.numpy as jnp
from jax import lax
from jax.experimental import pallas as pl
from jax.experimental.pallas import tpu as pltpu
from jax.sharding import PartitionSpec as P

NEWTON = 2
GATHERS = 1 + 2 * NEWTON
SPREADS = 2 * NEWTON + 1
PARTS = 3
MESH = pl.DeviceIdType.MESH


def arctan(x):
    size = jnp.abs(x)
    large = size > 2.414213562373095
    middle = size > 0.4142135623730950
    top = jnp.where(large, -1.0, jnp.where(middle, size - 1.0, size))
    bottom = jnp.where(large, size, jnp.where(middle, size + 1.0, 1.0))
    base = jnp.where(large, 1.5707963267948966, jnp.where(middle, 0.7853981633974483, 0.0))
    y = top / bottom
    z = y * y
    poly = ((8.05374449538e-2 * z - 1.38776856032e-1) * z + 1.99777106478e-1) * z - 3.33329491539e-1
    result = base + (poly * z * y + y)
    return jnp.where(x < 0.0, -result, result)


def split(x):
    parts = []
    for _ in range(PARTS):
        part = x.astype(jnp.bfloat16)
        parts.append(part)
        x = x - part.astype(jnp.float32)
    return jnp.concatenate(parts, axis=0)


def joined(x):
    rows = x.shape[0] // PARTS
    total = x[:rows]
    for k in range(1, PARTS):
        total = total + x[k * rows:(k + 1) * rows]
    return total


def lanes(row):
    return jnp.concatenate(
        [row[:, k * 128:(k + 1) * 128] for k in range(row.shape[1] // 128)], axis=0
    )


def flat(block):
    return jnp.concatenate([block[k:k + 1] for k in range(block.shape[0])], axis=1)


def partial_sum(x):
    x = jnp.sum(x, axis=0, keepdims=True)
    return jnp.sum(lanes(x), axis=0, keepdims=True)


def whole_sum(x):
    return jnp.sum(x, axis=1, keepdims=True)


def operator(field, shift):
    rows, width = field.shape
    row = lax.broadcasted_iota(jnp.int32, field.shape, 0)
    col = lax.broadcasted_iota(jnp.int32, field.shape, 1)
    up = jnp.where(row == 0, 0.0, pltpu.roll(field, 1, 0))
    down = jnp.where(row == rows - 1, 0.0, pltpu.roll(field, rows - 1, 0))
    left = jnp.where(col == 0, 0.0, pltpu.roll(field, 1, 1))
    right = jnp.where(col == width - 1, 0.0, pltpu.roll(field, width - 1, 1))
    return (4.0 + shift) * field - (up + down + left + right)


def kernel(
    n, heat_ref, start_ref, shift_ref, slave_ref, master_ref, d_ref, m_ref, cond_ref, active_ref,
    temp_ref, final_ref,
    hot, select, faces, kt, r0, kr0, r1, kr1,
    gbuf, hsend_buf, hrecv_buf, csend_buf, crecv_buf, fbuf,
    gsend, grecv, hsend, hrecv, csend, crecv, fsend, frecv,
):
    rows, width = heat_ref.shape
    pairs = slave_ref.shape[1]
    q = width // 128
    me = lax.axis_index("sub")
    group = lax.axis_index("groups")

    def device(j):
        return (group, lax.rem(me + j, n))

    barrier = pltpu.get_barrier_semaphore()

    def greet(j, carry):
        pl.semaphore_signal(barrier, inc=1, device_id=device(j), device_id_type=MESH)
        return carry

    lax.fori_loop(1, n, greet, 0)

    def tables():
        node = lax.broadcasted_iota(jnp.int32, (128, pairs), 0)
        block = lax.broadcasted_iota(jnp.int32, (n * q, pairs), 0)
        for k, (ref, weight) in enumerate(((slave_ref, d_ref[...]), (master_ref, -m_ref[...]))):
            face = ref[...]
            low = jnp.bitwise_and(face, 127)
            high = jnp.right_shift(face, 7)
            here = pl.ds(k * pairs, pairs)
            hot[:, here] = jnp.where(node == low, 1.0, 0.0).astype(jnp.bfloat16)
            select[:, here] = jnp.where(block == high, weight, 0.0)

    tables()
    pl.semaphore_wait(barrier, n - 1)

    def send_all(source, target, send_sem, recv_sem):
        def send(j, carry):
            to = lax.rem(me + j, n)
            pltpu.make_async_remote_copy(
                src_ref=source(to), dst_ref=target, send_sem=send_sem, recv_sem=recv_sem,
                device_id=(group, to), device_id_type=MESH,
            ).start()
            return carry

        lax.fori_loop(1, n, send, 0)

    def wait_all(buffer, sem):
        part = buffer.at[pl.ds(0, n - 1)]
        pltpu.make_async_copy(part, part, sem).wait()

    def gather_start(k, field, partial):
        gbuf[k, me, 0:q] = lanes(field[0:1])
        if partial is not None:
            gbuf[k, me, q:q + 1] = partial
        hsend_buf[k, 0:q] = lanes(field[rows - 1:rows])
        send_all(lambda to: gbuf.at[k, me], gbuf.at[k, me], gsend.at[k], grecv.at[k])
        halo_copy(k).start()

    def halo_copy(k):
        return pltpu.make_async_remote_copy(
            src_ref=hsend_buf.at[k], dst_ref=hrecv_buf.at[k], send_sem=hsend.at[k],
            recv_sem=hrecv.at[k], device_id=device(1), device_id_type=MESH,
        )

    def gather_end(k, partial):
        wait_all(gbuf.at[k], grecv.at[k])
        halo_copy(k).wait_recv()
        for j in range(n):
            faces[j * q:(j + 1) * q] = gbuf[k, j, 0:q]
        values = joined(
            jnp.dot(split(faces[...]), hot[...], preferred_element_type=jnp.float32)
        )
        ends = jnp.sum(values * select[...], axis=0, keepdims=True)
        gap = ends[:, :pairs] + ends[:, pairs:]
        above = jnp.where(me == 0, 0.0, flat(hrecv_buf[k, 0:q]))
        below = gbuf[k, lax.rem(me + 1, n), 0:q]
        below = jnp.where(me == n - 1, 0.0, flat(below))
        if partial:
            return gap, above, below, whole_sum(jnp.sum(gbuf[k, :, q:q + 1], axis=0))
        return gap, above, below

    def spread_start(k, flux, partial):
        weighted = select[...] * jnp.concatenate([flux, flux], axis=1)
        total = joined(
            lax.dot_general(
                split(weighted), hot[...], (((1,), (1,)), ((), ())),
                preferred_element_type=jnp.float32,
            )
        )
        for j in range(n):
            csend_buf[k, j, 0:q] = total[j * q:(j + 1) * q]
            if partial is not None:
                csend_buf[k, j, q:q + 1] = partial
        send_all(lambda to: csend_buf.at[k, to], crecv_buf.at[k, me], csend.at[k], crecv.at[k])
        crecv_buf[k, me, 0:q + 1] = csend_buf[k, me, 0:q + 1]

    def spread_end(k, partial):
        wait_all(crecv_buf.at[k], crecv.at[k])
        lift = flat(jnp.sum(crecv_buf[k, :, 0:q], axis=0))
        if partial:
            return lift, whole_sum(jnp.sum(crecv_buf[k, :, q:q + 1], axis=0))
        return lift

    def with_halo(ref, above, below):
        ref[0:1] = ref[0:1] - above
        ref[rows - 1:rows] = ref[rows - 1:rows] - below

    shift = shift_ref[...]
    live = active_ref[...].astype(jnp.float32) * cond_ref[...]

    gather_start(0, start_ref, None)
    kt[...] = operator(start_ref[...], shift) - heat_ref[...]
    gap_t, above, below = gather_end(0, False)
    with_halo(kt, above, below)
    for newton in range(NEWTON):
        first, second = 1 + 2 * newton, 2 + 2 * newton
        flux = live * (2.0 * gap_t - arctan(gap_t))
        spread_start(2 * newton, flux, None)
        slope = live * (2.0 - 1.0 / (1.0 + gap_t * gap_t))
        r0[...] = -kt[...]
        lift = spread_end(2 * newton, False)
        r0[0:1] = r0[0:1] - lift

        gather_start(first, r0, partial_sum(r0[...] * r0[...]))
        kr0[...] = operator(r0[...], shift)
        gap_0, above, below, rr = gather_end(first, True)
        with_halo(kr0, above, below)

        push = slope * gap_0
        spread_start(
            2 * newton + 1, push, partial_sum(r0[...] * kr0[...]) + partial_sum(push * gap_0)
        )
        lift, curve = spread_end(2 * newton + 1, True)
        alpha = rr / curve
        r1[...] = r0[...] - alpha * kr0[...]
        r1[0:1] = r1[0:1] - alpha * lift

        gather_start(second, r1, partial_sum(r1[...] * r1[...]))
        kr1[...] = operator(r1[...], shift)
        gap_1, above, below, rr_next = gather_end(second, True)
        with_halo(kr1, above, below)
        beta = rr_next / rr
        r1[...] = r1[...] + beta * r0[...]
        kr1[...] = kr1[...] + beta * kr0[...]
        gap_1 = gap_1 + beta * gap_0
        fbuf[newton, me] = partial_sum(r1[...] * kr1[...]) + partial_sum(slope * gap_1 * gap_1)
        send_all(
            lambda to: fbuf.at[newton, me], fbuf.at[newton, me], fsend.at[newton], frecv.at[newton]
        )
        temp = start_ref if newton == 0 else temp_ref
        temp_ref[...] = temp[...] + alpha * r0[...]
        kt[...] = kt[...] + alpha * kr0[...]
        wait_all(fbuf.at[newton], frecv.at[newton])
        alpha_next = rr_next / whole_sum(jnp.sum(fbuf[newton], axis=0))
        temp_ref[...] = temp_ref[...] + alpha_next * r1[...]
        kt[...] = kt[...] + alpha_next * kr1[...]
        gap_t = gap_t + alpha * gap_0 + alpha_next * gap_1

    flux = live * (2.0 * gap_t - arctan(gap_t))
    spread_start(2 * NEWTON, flux, None)
    final_ref[...] = kt[...]
    lift = spread_end(2 * NEWTON, False)
    final_ref[0:1] = final_ref[0:1] + lift

    for k in range(GATHERS):
        wait_all(gbuf.at[k], gsend.at[k])
        halo_copy(k).wait_send()
    for k in range(SPREADS):
        wait_all(csend_buf.at[k], csend.at[k])
    for k in range(NEWTON):
        wait_all(fbuf.at[k], fsend.at[k])


def on_device(heat, start, shift, slave, master, d_weight, m_weight, gap_cond, active):
    n = lax.axis_size("sub")
    rows, width = heat.shape
    pairs = slave.shape[0]
    q = width // 128
    tall = (q + 1 + 7) // 8 * 8
    field = pltpu.VMEM((rows, width), jnp.float32)
    sems = lambda count: pltpu.SemaphoreType.DMA((count,))
    vmem = pl.BlockSpec(memory_space=pltpu.VMEM)
    across = lambda x: x.reshape(1, pairs)
    return pl.pallas_call(
        functools.partial(kernel, n),
        out_shape=(jax.ShapeDtypeStruct((rows, width), jnp.float32),) * 2,
        in_specs=[vmem] * 9,
        out_specs=(vmem, vmem),
        scratch_shapes=[
            pltpu.VMEM((128, 2 * pairs), jnp.bfloat16),
            pltpu.VMEM((n * q, 2 * pairs), jnp.float32),
            pltpu.VMEM((n * q, 128), jnp.float32),
            field, field, field, field, field,
            pltpu.VMEM((GATHERS, n, tall, 128), jnp.float32),
            pltpu.VMEM((GATHERS, tall, 128), jnp.float32),
            pltpu.VMEM((GATHERS, tall, 128), jnp.float32),
            pltpu.VMEM((SPREADS, n, tall, 128), jnp.float32),
            pltpu.VMEM((SPREADS, n, tall, 128), jnp.float32),
            pltpu.VMEM((NEWTON, n, 1, 128), jnp.float32),
            sems(GATHERS), sems(GATHERS), sems(GATHERS), sems(GATHERS),
            sems(SPREADS), sems(SPREADS), sems(NEWTON), sems(NEWTON),
        ],
        compiler_params=pltpu.CompilerParams(
            collective_id=0, has_side_effects=True, vmem_limit_bytes=48 * 2**20
        ),
    )(
        heat, start, shift, across(slave), across(master), across(d_weight), across(m_weight),
        across(gap_cond), across(active),
    )


def solution(mesh):
    field = P(("groups", "sub"), None)
    pair = P(("groups", "sub"))
    return jax.shard_map(
        on_device, mesh=mesh, in_specs=(field,) * 3 + (pair,) * 6, out_specs=(field, field),
        check_vma=False,
    )
```

time: 951 us -> 72.2 us (0.08)
  blocking collectives: 724 us -> 0 us
  other arithmetic: 98.7 us -> 0 us
  local copies, waits for them, and re-layouts: 91.8 us -> 8.14 us
  Pallas kernels: 0 us -> 62.9 us
  starting transfers between devices: 25 us -> 0 us
    unnamed x7 -> x0, blocking collectives: 405 us -> none
    psum x6 -> x0, blocking collectives: 181 us -> none  [the longest x4 120 us: squares(): return lax.psum(jnp.sum(resvec * resvec), 'sub')]
    all_gather x7 -> x0, blocking collectives: 139 us -> none  [contact_terms(): faces = lax.all_gather(field_row, 'sub', axis=0, tiled=True)]
    gather x14 -> x0, local copies, waits for them, and re-layouts: 86.1 us -> none  [contact_terms(): gap = d_weight * faces[slave_face] - m_weight * faces[master_face]]
    scatter-add x14 -> x0, other arithmetic: 84.4 us -> none  [the longest x7 42.8 us: contact_terms(): total = total.at[master_face].add(-m_weight * weights)]
    pallas_call x0 -> x1, Pallas kernels: none -> 62.9 us  [on_device(): pl.pallas_call(functools.partial(kernel, n), out_shape=(jax.ShapeDtypeStr...]
    ppermute x14 -> x0, starting transfers between devices: 25 us -> none  [the longest x7 16 us: with_halo(): lax.ppermute(lax.slice_in_dim(block, block.shape[dim] - width, None, axis...]
  transfers between devices with their start and end apart: 14 -> 0, of which waited for: 0 -> 0; matrix products, arithmetic and copies ran while one was open for 18% -> 0% of each run, Pallas kernels for 0% -> 0%
where the time goes in v1:
time: 72.2 us; the launch traced here: 71.8 us
  Pallas kernels  62.9 us (87%)
  local copies, waits for them, and re-layouts  8.14 us (11%)
    pallas_call x1, Pallas kernels, on_device(): pl.pallas_call(functools.partial(kernel, n), out_shape=(jax.ShapeDtypeStr...  62.9 us
    unnamed x20, local copies, waits for them, and re-layouts  8.14 us

profile of v1, /device:TPU:0, one launch (start us, length us, event | category | flops | bytes accessed | tf_op | source)
XLA Modules:
  0.0 71.8 jit_solution(17100556730159045832)
XLA Ops:
  0.6 0.0 copy-start.4
  0.6 0.0 copy-start.3
  0.7 0.7 copy-done.4
  1.3 0.0 copy-done.3
  1.3 0.0 copy-start
  1.3 1.0 %copy-done = f32[256,512]{1,0:T(8,128)S(1)} copy-done((f32[256,512]{1,0:T(8,128)S(1)}, f32[256,512]{1,0:T(8,128)}, u32[]{:S(2)}) %copy-start) | copy-done | bytes 524312
  2.4 0.0 copy-start.1
  2.4 1.0 %copy-done.1 = f32[256,512]{1,0:T(8,128)S(1)} copy-done((f32[256,512]{1,0:T(8,128)S(1)}, f32[256,512]{1,0:T(8,128)}, u32[]{:S(2)}) %copy-start.1) | copy-done | bytes 524312
  3.4 0.0 copy-start.2
  3.4 1.0 %copy-done.2 = f32[256,512]{1,0:T(8,128)S(1)} copy-done((f32[256,512]{1,0:T(8,128)S(1)}, f32[256,512]{1,0:T(8,128)}, u32[]{:S(2)}) %copy-start.2) | copy-done | bytes 524312
  4.5 0.0 copy-start.5
  4.5 0.7 copy-done.5
  5.2 0.0 copy-start.6
  5.2 0.7 copy-done.6
  5.8 0.0 copy-start.7
  5.8 0.7 copy-done.7
  6.5 0.0 copy-start.8
  6.5 0.7 copy-done.8
  7.2 62.9 %shard_map.104 = (f32[256,512]{1,0:T(8,128)S(1)}, f32[256,512]{1,0:T(8,128)S(1)}) custom-call(f32[256,512]{1,0:T(8,128)S(1)} %copy-done, f32[256,512]{1,0:T(8,128)S(1)} %copy-done.1, f32[256,512]{1,0:T(8,128)S(1)} %copy-done.2, s32[1,1024]{1,0:T(1,128)S(1)} %bitcast.6, s32[1,1024]{1,0:T(1,128)S(1)} %bitcast.7, f32[1,1024]{1,0:T(1,128)S(1)} %bitcast.8, ...), custom_call_target="tpu_custom_call" | custom-call | tf_op jit(solution)/shard_map/pallas_call | solution.py:264
  70.2 0.8 %copy.13 = f32[256,512]{1,0:T(8,128)} copy(f32[256,512]{1,0:T(8,128)S(1)} %get-tuple-element.4) | data formatting | bytes 1048576
  71.0 0.8 %copy.14 = f32[256,512]{1,0:T(8,128)} copy(f32[256,512]{1,0:T(8,128)S(1)} %get-tuple-element.5) | data formatting | bytes 1048576
Async XLA Ops:
  0.6 0.7 copy-start.4
  0.6 0.7 copy-start.3
  1.3 1.0 %copy-start = (f32[256,512]{1,0:T(8,128)S(1)}, f32[256,512]{1,0:T(8,128)}, u32[]{:S(2)}) copy-start(f32[256,512]{1,0:T(8,128)} %heat_ref.1) | copy-start | bytes 1572868
  2.4 1.0 %copy-start.1 = (f32[256,512]{1,0:T(8,128)S(1)}, f32[256,512]{1,0:T(8,128)}, u32[]{:S(2)}) copy-start(f32[256,512]{1,0:T(8,128)} %start_ref.1) | copy-start | bytes 1572868
  3.4 1.0 %copy-start.2 = (f32[256,512]{1,0:T(8,128)S(1)}, f32[256,512]{1,0:T(8,128)}, u32[]{:S(2)}) copy-start(f32[256,512]{1,0:T(8,128)} %shift_ref.1) | copy-start | bytes 1572868
  4.5 0.7 copy-start.5
  5.2 0.7 copy-start.6
  5.8 0.7 copy-start.7
  6.5 0.7 copy-start.8

commit v2 on v1

v2 whole, which is shorter than its diff:
```python
import functools

import jax
import jax.numpy as jnp
from jax import lax
from jax.experimental import pallas as pl
from jax.experimental.pallas import tpu as pltpu
from jax.sharding import PartitionSpec as P

NEWTON = 2
GATHERS = 1 + 2 * NEWTON
PARTS = 3
MESH = pl.DeviceIdType.MESH


def arctan(x):
    size = jnp.abs(x)
    large = size > 2.414213562373095
    middle = size > 0.4142135623730950
    top = jnp.where(large, -1.0, jnp.where(middle, size - 1.0, size))
    bottom = jnp.where(large, size, jnp.where(middle, size + 1.0, 1.0))
    base = jnp.where(large, 1.5707963267948966, jnp.where(middle, 0.7853981633974483, 0.0))
    y = top / bottom
    z = y * y
    poly = ((8.05374449538e-2 * z - 1.38776856032e-1) * z + 1.99777106478e-1) * z - 3.33329491539e-1
    result = base + (poly * z * y + y)
    return jnp.where(x < 0.0, -result, result)


def split(x, count):
    parts = []
    for _ in range(count):
        part = x.astype(jnp.bfloat16).astype(jnp.float32)
        parts.append(part)
        x = x - part
    return jnp.concatenate(parts, axis=0).astype(jnp.bfloat16)


def joined(x, count):
    rows = x.shape[0] // count
    total = x[:rows]
    for k in range(1, count):
        total = total + x[k * rows:(k + 1) * rows]
    return total


def lanes(row):
    return jnp.concatenate(
        [row[:, k * 128:(k + 1) * 128] for k in range(row.shape[1] // 128)], axis=0
    )


def flat(block):
    return jnp.concatenate([block[k:k + 1] for k in range(block.shape[0])], axis=1)


def partial_sum(x):
    x = jnp.sum(x, axis=0, keepdims=True)
    return jnp.sum(lanes(x), axis=0, keepdims=True)


def whole_sum(x):
    return jnp.sum(x, axis=1, keepdims=True)


def operator(field, shift):
    rows, width = field.shape
    row = lax.broadcasted_iota(jnp.int32, field.shape, 0)
    col = lax.broadcasted_iota(jnp.int32, field.shape, 1)
    up = jnp.where(row == 0, 0.0, pltpu.roll(field, 1, 0))
    down = jnp.where(row == rows - 1, 0.0, pltpu.roll(field, rows - 1, 0))
    left = jnp.where(col == 0, 0.0, pltpu.roll(field, 1, 1))
    right = jnp.where(col == width - 1, 0.0, pltpu.roll(field, width - 1, 1))
    return (4.0 + shift) * field - (up + down + left + right)


def kernel(
    n, heat_ref, start_ref, shift_ref, slave_ref, master_ref, d_ref, m_ref, cond_ref, active_ref,
    temp_ref, final_ref,
    hot_own, hot_other, pick_own, pick_other, faces, kt, r0, kr0, w0, kw0, r1,
    gbuf, hsend_buf, hrecv_buf, rsend_buf, rrecv_buf, fbuf,
    gsend, grecv, hsend, hrecv, rsend, rrecv, fsend, frecv,
):
    rows, width = heat_ref.shape
    pairs = slave_ref.shape[1]
    q = width // 128
    slots = rsend_buf.shape[2]
    listed = hot_own.shape[1]
    me = lax.axis_index("sub")
    group = lax.axis_index("groups")

    def device(j):
        return (group, lax.rem(me + j, n))

    barrier = pltpu.get_barrier_semaphore()

    def greet(j, carry):
        pl.semaphore_signal(barrier, inc=1, device_id=device(j), device_id_type=MESH)
        return carry

    lax.fori_loop(1, n, greet, 0)

    def send_all(source, target, send_sem, recv_sem):
        def send(j, carry):
            to = lax.rem(me + j, n)
            pltpu.make_async_remote_copy(
                src_ref=source(to), dst_ref=target, send_sem=send_sem, recv_sem=recv_sem,
                device_id=(group, to), device_id_type=MESH,
            ).start()
            return carry

        lax.fori_loop(1, n, send, 0)

    def wait_all(buffer, sem):
        part = buffer.at[pl.ds(0, n - 1)]
        pltpu.make_async_copy(part, part, sem).wait()

    def records():
        slave, master = slave_ref[...], master_ref[...]
        d, m = d_ref[...], -m_ref[...]
        live = active_ref[...].astype(jnp.float32) * cond_ref[...]
        log = width.bit_length() - 1
        block = lax.broadcasted_iota(jnp.int32, (n, pairs), 0)
        upto = lax.broadcasted_iota(jnp.int32, (128, 128), 0) <= lax.broadcasted_iota(
            jnp.int32, (128, 128), 1
        )
        upto = jnp.where(upto, 1.0, 0.0).astype(jnp.bfloat16)
        slot = lax.broadcasted_iota(jnp.int32, (slots, pairs), 0)
        owners, fields, places = [], [], []
        for own, other, mine, theirs in ((slave, master, d, m), (master, slave, m, d)):
            owner = jnp.right_shift(own, log)
            named = jnp.where(block == owner, 1.0, 0.0)
            chunks = [named[:, k:k + 128] for k in range(0, pairs, 128)]
            counts = jnp.dot(
                jnp.concatenate(chunks, axis=0).astype(jnp.bfloat16), upto,
                preferred_element_type=jnp.float32,
            )
            before = jnp.zeros((n, 1), jnp.float32)
            ranks = []
            for k, chunk in enumerate(chunks):
                count = counts[k * n:(k + 1) * n] + before
                before = count[:, 127:128]
                ranks.append(jnp.sum(count * chunk, axis=0, keepdims=True) - 1.0)
            rank = jnp.concatenate(ranks, axis=1).astype(jnp.int32)
            places.append(jnp.where(slot == rank, 1.0, 0.0).astype(jnp.bfloat16))
            code = other * width + jnp.bitwise_and(own, width - 1)
            fields += [code.astype(jnp.float32), mine, theirs, live]
            owners += [owner] * 4
        fields = jnp.concatenate(fields, axis=0)[None]
        owners = jnp.concatenate(owners, axis=0)[None]
        block = lax.broadcasted_iota(jnp.int32, (n, 8, pairs), 0)
        spread = jnp.where(block == owners, fields, 0.0).reshape(8 * n, pairs)
        placed = joined(
            lax.dot_general(
                split(spread, 3), jnp.concatenate(places, axis=0), (((1,), (1,)), ((), ())),
                preferred_element_type=jnp.float32,
            ),
            3,
        )
        row = jnp.bitwise_and(lax.broadcasted_iota(jnp.int32, (8 * n, slots), 0), 7)
        placed = jnp.where(row < 4, placed[:, :slots], placed[:, slots:])
        rsend_buf[...] = placed.reshape(n, 8, slots)

    def field_of(k):
        return jnp.concatenate(
            [rrecv_buf[j, k + role:k + role + 1] for role in (0, 4) for j in range(n)], axis=1
        )

    def tables():
        code = field_of(0).astype(jnp.int32)
        own = jnp.bitwise_and(code, width - 1)
        other = jnp.right_shift(code, width.bit_length() - 1)
        node = lax.broadcasted_iota(jnp.int32, (128, listed), 0)
        for hot, face, pick, weight in (
            (hot_own, own, pick_own, field_of(1)), (hot_other, other, pick_other, field_of(2))
        ):
            low, high = jnp.bitwise_and(face, 127), jnp.right_shift(face, 7)
            hot[...] = jnp.where(node == low, 1.0, 0.0).astype(jnp.bfloat16)
            block = lax.broadcasted_iota(jnp.int32, pick.shape, 0)
            pick[...] = jnp.where(block == high, weight, 0.0)
        return field_of(3)

    def ends(rows_of, hot, pick):
        parts = split(rows_of, PARTS)
        pieces = []
        step = min(listed, 2048)
        for k in range(0, listed, step):
            here = pl.ds(k, step)
            values = joined(
                jnp.dot(parts, hot[:, here], preferred_element_type=jnp.float32), PARTS
            )
            pieces.append(jnp.sum(values * pick[:, here], axis=0, keepdims=True))
        return jnp.concatenate(pieces, axis=1)

    def lift_of(flux):
        total = joined(
            lax.dot_general(
                split(pick_own[...] * flux, PARTS), hot_own[...], (((1,), (1,)), ((), ())),
                preferred_element_type=jnp.float32,
            ),
            PARTS,
        )
        return flat(total[0:q])

    def gather_start(k, field, partial):
        gbuf[k, me, 0:q] = lanes(field[0:1])
        if partial is not None:
            gbuf[k, me, q:q + 1] = partial
        hsend_buf[k, 0:q] = lanes(field[rows - 1:rows])
        send_all(lambda to: gbuf.at[k, me], gbuf.at[k, me], gsend.at[k], grecv.at[k])
        halo_copy(k).start()

    def halo_copy(k):
        return pltpu.make_async_remote_copy(
            src_ref=hsend_buf.at[k], dst_ref=hrecv_buf.at[k], send_sem=hsend.at[k],
            recv_sem=hrecv.at[k], device_id=device(1), device_id_type=MESH,
        )

    def own_ends(field):
        own = jnp.concatenate(
            [lanes(field[0:1]), jnp.zeros((pick_own.shape[0] - q, 128), jnp.float32)], axis=0
        )
        return ends(own, hot_own, pick_own)

    def gather_end(k):
        wait_all(gbuf.at[k], grecv.at[k])
        halo_copy(k).wait_recv()
        for j in range(n):
            faces[j * q:(j + 1) * q] = gbuf[k, j, 0:q]

    def halos(k, ref):
        above = jnp.where(me == 0, 0.0, flat(hrecv_buf[k, 0:q]))
        below = gbuf[k, lax.rem(me + 1, n), 0:q]
        below = jnp.where(me == n - 1, 0.0, flat(below))
        ref[0:1] = ref[0:1] - above
        ref[rows - 1:rows] = ref[rows - 1:rows] - below

    def total_of(k):
        return whole_sum(jnp.sum(gbuf[k, :, q:q + 1], axis=0))

    shift = shift_ref[...]
    records()
    pl.semaphore_wait(barrier, n - 1)
    send_all(lambda to: rsend_buf.at[to], rrecv_buf.at[me], rsend.at[0], rrecv.at[0])
    gather_start(0, start_ref, None)
    rrecv_buf[me] = rsend_buf[me]
    kt[...] = operator(start_ref[...], shift) - heat_ref[...]
    wait_all(rrecv_buf, rrecv.at[0])
    live = tables()
    gather_end(0)
    halos(0, kt)
    gap_t = own_ends(start_ref) + ends(faces[...], hot_other, pick_other)

    for newton in range(NEWTON):
        first, second = 1 + 2 * newton, 2 + 2 * newton
        lift = lift_of(live * (2.0 * gap_t - arctan(gap_t)))
        r0[...] = -kt[...]
        r0[0:1] = r0[0:1] - lift

        gather_start(first, r0, partial_sum(r0[...] * r0[...]))
        kr0[...] = operator(r0[...], shift)
        slope = live * (2.0 - 1.0 / (1.0 + gap_t * gap_t))
        gap_0 = own_ends(r0)
        gather_end(first)
        halos(first, kr0)
        gap_0 = gap_0 + ends(faces[...], hot_other, pick_other)
        lift = lift_of(slope * gap_0)
        w0[...] = kr0[...]
        w0[0:1] = w0[0:1] + lift

        gather_start(second, w0, partial_sum(r0[...] * w0[...]))
        rr = total_of(first)
        kw0[...] = operator(w0[...], shift)
        gap_w = own_ends(w0)
        gather_end(second)
        halos(second, kw0)
        curve = total_of(second)
        alpha = rr / curve
        gap_w = gap_w + ends(faces[...], hot_other, pick_other)
        lift = lift_of(slope * gap_w)
        r1[...] = r0[...] - alpha * w0[...]
        residual = r1[...]
        fbuf[newton, me, 0:1] = partial_sum(residual * residual)
        fbuf[newton, me, 1:2] = partial_sum(residual * w0[...])
        fbuf[newton, me, 2:3] = partial_sum(
            residual * (w0[...] - alpha * kw0[...])
        ) - alpha * partial_sum(residual[0:1] * lift)
        send_all(
            lambda to: fbuf.at[newton, me], fbuf.at[newton, me], fsend.at[newton], frecv.at[newton]
        )
        temp = start_ref if newton == 0 else temp_ref
        temp_ref[...] = temp[...] + alpha * r0[...]
        kt[...] = kt[...] + alpha * kr0[...]
        gap_t = gap_t + alpha * gap_0
        gap_1 = gap_0 - alpha * gap_w
        wait_all(fbuf.at[newton], frecv.at[newton])
        sums = whole_sum(jnp.sum(fbuf[newton], axis=0))
        rr_next, cross, inner = sums[0:1], sums[1:2], sums[2:3]
        beta = rr_next / rr
        alpha_next = rr_next / (inner + 2.0 * beta * cross + beta * beta * curve)
        gap_t = gap_t + alpha_next * (gap_1 + beta * gap_0)
        kt[...] = kt[...] + alpha_next * (kr0[...] - alpha * kw0[...] + beta * kr0[...])
        temp_ref[...] = temp_ref[...] + alpha_next * (r1[...] + beta * r0[...])

    lift = lift_of(live * (2.0 * gap_t - arctan(gap_t)))
    final_ref[...] = kt[...]
    final_ref[0:1] = final_ref[0:1] + lift

    for k in range(GATHERS):
        wait_all(gbuf.at[k], gsend.at[k])
        halo_copy(k).wait_send()
    wait_all(rsend_buf, rsend.at[0])
    for k in range(NEWTON):
        wait_all(fbuf.at[k], fsend.at[k])


def on_device(heat, start, shift, slave, master, d_weight, m_weight, gap_cond, active):
    n = lax.axis_size("sub")
    rows, width = heat.shape
    pairs = slave.shape[0]
    q = width // 128
    slots = pairs // 8
    listed = 2 * n * slots
    tall = (q + 1 + 7) // 8 * 8
    own_rows = (q + 7) // 8 * 8
    field = pltpu.VMEM((rows, width), jnp.float32)
    sems = lambda count: pltpu.SemaphoreType.DMA((count,))
    vmem = pl.BlockSpec(memory_space=pltpu.VMEM)
    across = lambda x: x.reshape(1, pairs)
    return pl.pallas_call(
        functools.partial(kernel, n),
        out_shape=(jax.ShapeDtypeStruct((rows, width), jnp.float32),) * 2,
        in_specs=[vmem] * 9,
        out_specs=(vmem, vmem),
        scratch_shapes=[
            pltpu.VMEM((128, listed), jnp.bfloat16),
            pltpu.VMEM((128, listed), jnp.bfloat16),
            pltpu.VMEM((own_rows, listed), jnp.float32),
            pltpu.VMEM((n * q, listed), jnp.float32),
            pltpu.VMEM((n * q, 128), jnp.float32),
            field, field, field, field, field, field,
            pltpu.VMEM((GATHERS, n, tall, 128), jnp.float32),
            pltpu.VMEM((GATHERS, tall, 128), jnp.float32),
            pltpu.VMEM((GATHERS, tall, 128), jnp.float32),
            pltpu.VMEM((n, 8, slots), jnp.float32),
            pltpu.VMEM((n, 8, slots), jnp.float32),
            pltpu.VMEM((NEWTON, n, 8, 128), jnp.float32),
            sems(GATHERS), sems(GATHERS), sems(GATHERS), sems(GATHERS),
            sems(1), sems(1), sems(NEWTON), sems(NEWTON),
        ],
        compiler_params=pltpu.CompilerParams(
            collective_id=0, has_side_effects=True, vmem_limit_bytes=48 * 2**20
        ),
    )(
        heat, start, shift, across(slave), across(master), across(d_weight), across(m_weight),
        across(gap_cond), across(active),
    )


def solution(mesh):
    field = P(("groups", "sub"), None)
    pair = P(("groups", "sub"))
    return jax.shard_map(
        on_device, mesh=mesh, in_specs=(field,) * 3 + (pair,) * 6, out_specs=(field, field),
        check_vma=False,
    )
```

time: 72.2 us -> 53.2 us (0.74)
  Pallas kernels: 62.9 us -> 44 us
    pallas_call x1, Pallas kernels: 62.9 us -> 44 us  [on_device(): pl.pallas_call(functools.partial(kernel, n), out_shape=(jax.ShapeDtypeStr...]
where the time goes in v2:
time: 53.2 us; the launch traced here: 52.8 us
  Pallas kernels  44 us (83%)
  local copies, waits for them, and re-layouts  8.14 us (15%)
  between operations  0.67 us (1%)
    pallas_call x1, Pallas kernels, on_device(): pl.pallas_call(functools.partial(kernel, n), out_shape=(jax.ShapeDtypeStr...  44 us
    unnamed x20, local copies, waits for them, and re-layouts  8.14 us

profile of v2, /device:TPU:0, one launch (start us, length us, event | category | flops | bytes accessed | tf_op | source)
XLA Modules:
  0.0 52.8 jit_solution(14347957230510023887)
XLA Ops:
  0.6 0.0 copy-start.4
  0.6 0.0 copy-start.3
  0.7 0.7 %copy-done.4 = s32[1024]{0:T(1024)S(1)} copy-done((s32[1024]{0:T(1024)S(1)}, s32[1024]{0:T(1024)}, u32[]{:S(2)}) %copy-start.4) | copy-done | bytes 4120
  1.3 0.0 copy-done.3
  1.3 0.0 copy-start
  1.3 1.0 %copy-done = f32[256,512]{1,0:T(8,128)S(1)} copy-done((f32[256,512]{1,0:T(8,128)S(1)}, f32[256,512]{1,0:T(8,128)}, u32[]{:S(2)}) %copy-start) | copy-done | bytes 524312
  2.4 0.0 copy-start.1
  2.4 1.0 %copy-done.1 = f32[256,512]{1,0:T(8,128)S(1)} copy-done((f32[256,512]{1,0:T(8,128)S(1)}, f32[256,512]{1,0:T(8,128)}, u32[]{:S(2)}) %copy-start.1) | copy-done | bytes 524312
  3.4 0.0 copy-start.2
  3.4 1.0 %copy-done.2 = f32[256,512]{1,0:T(8,128)S(1)} copy-done((f32[256,512]{1,0:T(8,128)S(1)}, f32[256,512]{1,0:T(8,128)}, u32[]{:S(2)}) %copy-start.2) | copy-done | bytes 524312
  4.5 0.0 copy-start.5
  4.5 0.7 %copy-done.5 = f32[1024]{0:T(1024)S(1)} copy-done((f32[1024]{0:T(1024)S(1)}, f32[1024]{0:T(1024)}, u32[]{:S(2)}) %copy-start.5) | copy-done | bytes 4120
  5.2 0.0 copy-start.6
  5.2 0.7 %copy-done.6 = f32[1024]{0:T(1024)S(1)} copy-done((f32[1024]{0:T(1024)S(1)}, f32[1024]{0:T(1024)}, u32[]{:S(2)}) %copy-start.6) | copy-done | bytes 4120
  5.8 0.0 copy-start.7
  5.8 0.7 %copy-done.7 = f32[1024]{0:T(1024)S(1)} copy-done((f32[1024]{0:T(1024)S(1)}, f32[1024]{0:T(1024)}, u32[]{:S(2)}) %copy-start.7) | copy-done | bytes 4120
  6.5 0.0 copy-start.8
  6.5 0.7 %copy-done.8 = s32[1024]{0:T(1024)S(1)} copy-done((s32[1024]{0:T(1024)S(1)}, s32[1024]{0:T(1024)}, u32[]{:S(2)}) %copy-start.8) | copy-done | bytes 4120
  7.2 44.0 %shard_map.104 = (f32[256,512]{1,0:T(8,128)S(1)}, f32[256,512]{1,0:T(8,128)S(1)}) custom-call(f32[256,512]{1,0:T(8,128)S(1)} %copy-done, f32[256,512]{1,0:T(8,128)S(1)} %copy-done.1, f32[256,512]{1,0:T(8,128)S(1)} %copy-done.2, s32[1,1024]{1,0:T(1,128)S(1)} %bitcast.6, s32[1,1024]{1,0:T(1,128)S(1)} %bitcast.7, f32[1,1024]{1,0:T(1,128)S(1)} %bitcast.8, ...), custom_call_target="tpu_custom_call" | custom-call | tf_op jit(solution)/shard_map/pallas_call | solution.py:330
  51.2 0.8 %copy.13 = f32[256,512]{1,0:T(8,128)} copy(f32[256,512]{1,0:T(8,128)S(1)} %get-tuple-element.4) | data formatting | bytes 1048576
  52.0 0.8 %copy.14 = f32[256,512]{1,0:T(8,128)} copy(f32[256,512]{1,0:T(8,128)S(1)} %get-tuple-element.5) | data formatting | bytes 1048576
Async XLA Ops:
  0.6 0.7 %copy-start.4 = (s32[1024]{0:T(1024)S(1)}, s32[1024]{0:T(1024)}, u32[]{:S(2)}) copy-start(s32[1024]{0:T(1024)} %param.13) | copy-start | bytes 12292
  0.6 0.7 %copy-start.3 = (s32[1024]{0:T(1024)S(1)}, s32[1024]{0:T(1024)}, u32[]{:S(2)}) copy-start(s32[1024]{0:T(1024)} %param.12) | copy-start | bytes 12292
  1.3 1.0 %copy-start = (f32[256,512]{1,0:T(8,128)S(1)}, f32[256,512]{1,0:T(8,128)}, u32[]{:S(2)}) copy-start(f32[256,512]{1,0:T(8,128)} %heat_ref.1) | copy-start | bytes 1572868
  2.4 1.0 %copy-start.1 = (f32[256,512]{1,0:T(8,128)S(1)}, f32[256,512]{1,0:T(8,128)}, u32[]{:S(2)}) copy-start(f32[256,512]{1,0:T(8,128)} %start_ref.1) | copy-start | bytes 1572868
  3.4 1.0 %copy-start.2 = (f32[256,512]{1,0:T(8,128)S(1)}, f32[256,512]{1,0:T(8,128)}, u32[]{:S(2)}) copy-start(f32[256,512]{1,0:T(8,128)} %shift_ref.1) | copy-start | bytes 1572868
  4.5 0.7 %copy-start.5 = (f32[1024]{0:T(1024)S(1)}, f32[1024]{0:T(1024)}, u32[]{:S(2)}) copy-start(f32[1024]{0:T(1024)} %param.14) | copy-start | bytes 12292
  5.2 0.7 %copy-start.6 = (f32[1024]{0:T(1024)S(1)}, f32[1024]{0:T(1024)}, u32[]{:S(2)}) copy-start(f32[1024]{0:T(1024)} %param.15) | copy-start | bytes 12292
  5.8 0.7 %copy-start.7 = (f32[1024]{0:T(1024)S(1)}, f32[1024]{0:T(1024)}, u32[]{:S(2)}) copy-start(f32[1024]{0:T(1024)} %param.16) | copy-start | bytes 12292
  6.5 0.7 %copy-start.8 = (s32[1024]{0:T(1024)S(1)}, s32[1024]{0:T(1024)}, u32[]{:S(2)}) copy-start(s32[1024]{0:T(1024)} %param.17) | copy-start | bytes 12292

commit v3 on v2

--- a/solution.py
+++ b/solution.py
@@ -9,7 +9,7 @@
 
 NEWTON = 2
 GATHERS = 1 + 2 * NEWTON
-PARTS = 3
+PARTS = 2
 MESH = pl.DeviceIdType.MESH
 
 
@@ -75,12 +75,23 @@
 
 
 def kernel(
-    n, heat_ref, start_ref, shift_ref, slave_ref, master_ref, d_ref, m_ref, cond_ref, active_ref,
+    n, heat_in, start_in, shift_in, slave_in, master_in, d_in, m_in, cond_in, active_in,
     temp_ref, final_ref,
-    hot_own, hot_other, pick_own, pick_other, faces, kt, r0, kr0, w0, kw0, r1,
-    gbuf, hsend_buf, hrecv_buf, rsend_buf, rrecv_buf, fbuf,
-    gsend, grecv, hsend, hrecv, rsend, rrecv, fsend, frecv,
+    heat_ref, start_ref, shift_ref, slave_ref, master_ref, d_ref, m_ref, cond_ref, active_ref,
+    hot_own, hot_other, pick_own, pick_other, faces, kt, r0, w0, kw0,
+    plain_buf, sums_buf, hsend_buf, hrecv_buf, rsend_buf, rrecv_buf, fbuf,
+    loads, gsend, grecv, hsend, hrecv, rsend, rrecv, fsend, frecv,
 ):
+    inputs = [
+        pltpu.make_async_copy(source, target, loads.at[k])
+        for k, (source, target) in enumerate((
+            (slave_in, slave_ref), (master_in, master_ref), (d_in, d_ref), (m_in, m_ref),
+            (cond_in, cond_ref), (active_in, active_ref), (start_in, start_ref),
+            (shift_in, shift_ref), (heat_in, heat_ref),
+        ))
+    ]
+    for copy in inputs:
+        copy.start()
     rows, width = heat_ref.shape
     pairs = slave_ref.shape[1]
     q = width // 128
@@ -202,12 +213,18 @@
         )
         return flat(total[0:q])
 
-    def gather_start(k, field, partial):
-        gbuf[k, me, 0:q] = lanes(field[0:1])
-        if partial is not None:
-            gbuf[k, me, q:q + 1] = partial
-        hsend_buf[k, 0:q] = lanes(field[rows - 1:rows])
-        send_all(lambda to: gbuf.at[k, me], gbuf.at[k, me], gsend.at[k], grecv.at[k])
+    def slab(k):
+        if k > 0 and k % 2 == 0:
+            return sums_buf.at[k // 2 - 1]
+        return plain_buf.at[(k + 1) // 2]
+
+    def gather_start(k, top, bottom, partials=()):
+        buffer = slab(k)
+        buffer[me, 0:q] = lanes(top)
+        for place, partial in enumerate(partials):
+            buffer[me, q + place:q + place + 1] = partial
+        hsend_buf[k] = lanes(bottom)
+        send_all(lambda to: buffer.at[me], buffer.at[me], gsend.at[k], grecv.at[k])
         halo_copy(k).start()
 
     def halo_copy(k):
@@ -216,98 +233,111 @@
             recv_sem=hrecv.at[k], device_id=device(1), device_id_type=MESH,
         )
 
-    def own_ends(field):
+    def own_ends(top):
         own = jnp.concatenate(
-            [lanes(field[0:1]), jnp.zeros((pick_own.shape[0] - q, 128), jnp.float32)], axis=0
+            [lanes(top), jnp.zeros((pick_own.shape[0] - q, 128), jnp.float32)], axis=0
         )
         return ends(own, hot_own, pick_own)
 
     def gather_end(k):
-        wait_all(gbuf.at[k], grecv.at[k])
+        buffer = slab(k)
+        wait_all(buffer, grecv.at[k])
         halo_copy(k).wait_recv()
         for j in range(n):
-            faces[j * q:(j + 1) * q] = gbuf[k, j, 0:q]
-
-    def halos(k, ref):
-        above = jnp.where(me == 0, 0.0, flat(hrecv_buf[k, 0:q]))
-        below = gbuf[k, lax.rem(me + 1, n), 0:q]
-        below = jnp.where(me == n - 1, 0.0, flat(below))
-        ref[0:1] = ref[0:1] - above
-        ref[rows - 1:rows] = ref[rows - 1:rows] - below
-
-    def total_of(k):
-        return whole_sum(jnp.sum(gbuf[k, :, q:q + 1], axis=0))
-
-    shift = shift_ref[...]
+            faces[j * q:(j + 1) * q] = buffer[j, 0:q]
+        above = jnp.where(me == 0, 0.0, flat(hrecv_buf[k]))
+        below = jnp.where(me == n - 1, 0.0, flat(buffer[lax.rem(me + 1, n), 0:q]))
+        return ends(faces[...], hot_other, pick_other), above, below
+
+    def lane_sum(row):
+        return jnp.sum(lanes(row), axis=0, keepdims=True)
+
+    first_row, last_row = pl.ds(0, 1), pl.ds(rows - 1, 1)
+
+    for copy in inputs[:6]:
+        copy.wait()
     records()
+    inputs[6].wait()
     pl.semaphore_wait(barrier, n - 1)
     send_all(lambda to: rsend_buf.at[to], rrecv_buf.at[me], rsend.at[0], rrecv.at[0])
-    gather_start(0, start_ref, None)
+    gather_start(0, start_ref[first_row], start_ref[last_row])
     rrecv_buf[me] = rsend_buf[me]
-    kt[...] = operator(start_ref[...], shift) - heat_ref[...]
+    inputs[7].wait()
+    inputs[8].wait()
+    kt[...] = operator(start_ref[...], shift_ref[...]) - heat_ref[...]
     wait_all(rrecv_buf, rrecv.at[0])
     live = tables()
-    gather_end(0)
-    halos(0, kt)
-    gap_t = own_ends(start_ref) + ends(faces[...], hot_other, pick_other)
+    gap_t = own_ends(start_ref[first_row])
+    gap_other, above, below = gather_end(0)
+    gap_t = gap_t + gap_other
+    kt[first_row] = kt[first_row] - above
+    kt[last_row] = kt[last_row] - below
+    top, bottom = -kt[first_row], -kt[last_row]
 
     for newton in range(NEWTON):
         first, second = 1 + 2 * newton, 2 + 2 * newton
-        lift = lift_of(live * (2.0 * gap_t - arctan(gap_t)))
+        top = top - lift_of(live * (2.0 * gap_t - arctan(gap_t)))
+        gather_start(first, top, bottom)
+        if newton > 0:
+            kt[...] = kt[...] + (step_0 * w0[...] + step_w * kw0[...])
+            kt[first_row] = kt[first_row] - step_0 * lift_0
+            temp_ref[...] = temp_ref[...] + (step_0 * r0[...] + step_w * w0[...])
+        else:
+            temp_ref[...] = start_ref[...]
         r0[...] = -kt[...]
-        r0[0:1] = r0[0:1] - lift
-
-        gather_start(first, r0, partial_sum(r0[...] * r0[...]))
-        kr0[...] = operator(r0[...], shift)
+        r0[first_row] = top
+        r0[last_row] = bottom
+        w0[...] = operator(r0[...], shift_ref[...])
+        squares = partial_sum(r0[...] * r0[...])
+        inner = partial_sum(r0[...] * w0[...])
         slope = live * (2.0 - 1.0 / (1.0 + gap_t * gap_t))
-        gap_0 = own_ends(r0)
-        gather_end(first)
-        halos(first, kr0)
-        gap_0 = gap_0 + ends(faces[...], hot_other, pick_other)
-        lift = lift_of(slope * gap_0)
-        w0[...] = kr0[...]
-        w0[0:1] = w0[0:1] + lift
-
-        gather_start(second, w0, partial_sum(r0[...] * w0[...]))
-        rr = total_of(first)
-        kw0[...] = operator(w0[...], shift)
-        gap_w = own_ends(w0)
-        gather_end(second)
-        halos(second, kw0)
-        curve = total_of(second)
+        gap_0 = own_ends(top)
+        gap_other, above, below = gather_end(first)
+        gap_0 = gap_0 + gap_other
+        lift_0 = lift_of(slope * gap_0)
+        w0[first_row] = w0[first_row] + (lift_0 - above)
+        w0[last_row] = w0[last_row] - below
+        inner = inner + lane_sum(top * (lift_0 - above) - bottom * below)
+
+        gather_start(second, w0[first_row], w0[last_row], (squares, inner))
+        kw0[...] = operator(w0[...], shift_ref[...])
+        gap_w = own_ends(w0[first_row])
+        gap_other, above, below = gather_end(second)
+        gap_w = gap_w + gap_other
+        lift_w = lift_of(slope * gap_w)
+        totals = whole_sum(jnp.sum(slab(second)[:, q:q + 2], axis=0))
+        rr, curve = totals[0:1], totals[1:2]
         alpha = rr / curve
-        gap_w = gap_w + ends(faces[...], hot_other, pick_other)
-        lift = lift_of(slope * gap_w)
-        r1[...] = r0[...] - alpha * w0[...]
-        residual = r1[...]
-        fbuf[newton, me, 0:1] = partial_sum(residual * residual)
-        fbuf[newton, me, 1:2] = partial_sum(residual * w0[...])
+        kw0[first_row] = kw0[first_row] - above
+        kw0[last_row] = kw0[last_row] - below
+        resid = r0[...] - alpha * w0[...]
+        fbuf[newton, me, 0:1] = partial_sum(resid * resid)
+        fbuf[newton, me, 1:2] = partial_sum(resid * w0[...])
         fbuf[newton, me, 2:3] = partial_sum(
-            residual * (w0[...] - alpha * kw0[...])
-        ) - alpha * partial_sum(residual[0:1] * lift)
+            resid * (w0[...] - alpha * kw0[...])
+        ) - alpha * lane_sum(resid[0:1] * lift_w)
         send_all(
             lambda to: fbuf.at[newton, me], fbuf.at[newton, me], fsend.at[newton], frecv.at[newton]
         )
-        temp = start_ref if newton == 0 else temp_ref
-        temp_ref[...] = temp[...] + alpha * r0[...]
-        kt[...] = kt[...] + alpha * kr0[...]
-        gap_t = gap_t + alpha * gap_0
-        gap_1 = gap_0 - alpha * gap_w
         wait_all(fbuf.at[newton], frecv.at[newton])
-        sums = whole_sum(jnp.sum(fbuf[newton], axis=0))
-        rr_next, cross, inner = sums[0:1], sums[1:2], sums[2:3]
+        totals = whole_sum(jnp.sum(fbuf[newton, :, 0:3], axis=0))
+        rr_next, cross, inner = totals[0:1], totals[1:2], totals[2:3]
         beta = rr_next / rr
         alpha_next = rr_next / (inner + 2.0 * beta * cross + beta * beta * curve)
-        gap_t = gap_t + alpha_next * (gap_1 + beta * gap_0)
-        kt[...] = kt[...] + alpha_next * (kr0[...] - alpha * kw0[...] + beta * kr0[...])
-        temp_ref[...] = temp_ref[...] + alpha_next * (r1[...] + beta * r0[...])
-
-    lift = lift_of(live * (2.0 * gap_t - arctan(gap_t)))
-    final_ref[...] = kt[...]
-    final_ref[0:1] = final_ref[0:1] + lift
+        step_0 = alpha + alpha_next * (1.0 + beta)
+        step_w = -(alpha_next * alpha)
+        gap_t = gap_t + (step_0 * gap_0 + step_w * gap_w)
+        top = -(
+            kt[first_row] + (step_0 * (w0[first_row] - lift_0) + step_w * kw0[first_row])
+        )
+        bottom = -(kt[last_row] + (step_0 * w0[last_row] + step_w * kw0[last_row]))
+
+    temp_ref[...] = temp_ref[...] + (step_0 * r0[...] + step_w * w0[...])
+    final_ref[...] = kt[...] + (step_0 * w0[...] + step_w * kw0[...])
+    final_ref[first_row] = lift_of(live * (2.0 * gap_t - arctan(gap_t))) - top
 
     for k in range(GATHERS):
-        wait_all(gbuf.at[k], gsend.at[k])
+        wait_all(slab(k), gsend.at[k])
         halo_copy(k).wait_send()
     wait_all(rsend_buf, rsend.at[0])
     for k in range(NEWTON):
@@ -321,40 +351,42 @@
     q = width // 128
     slots = pairs // 8
     listed = 2 * n * slots
-    tall = (q + 1 + 7) // 8 * 8
+    tall = (q + 2 + 7) // 8 * 8
     own_rows = (q + 7) // 8 * 8
     field = pltpu.VMEM((rows, width), jnp.float32)
+    whole = lambda x: pltpu.VMEM(x.shape, x.dtype)
     sems = lambda count: pltpu.SemaphoreType.DMA((count,))
     vmem = pl.BlockSpec(memory_space=pltpu.VMEM)
-    across = lambda x: x.reshape(1, pairs)
+    hbm = pl.BlockSpec(memory_space=pltpu.HBM)
+    operands = (heat, start, shift) + tuple(
+        x.reshape(1, pairs) for x in (slave, master, d_weight, m_weight, gap_cond, active)
+    )
     return pl.pallas_call(
         functools.partial(kernel, n),
         out_shape=(jax.ShapeDtypeStruct((rows, width), jnp.float32),) * 2,
-        in_specs=[vmem] * 9,
+        in_specs=[hbm] * 9,
         out_specs=(vmem, vmem),
-        scratch_shapes=[
+        scratch_shapes=[whole(x) for x in operands] + [
             pltpu.VMEM((128, listed), jnp.bfloat16),
             pltpu.VMEM((128, listed), jnp.bfloat16),
             pltpu.VMEM((own_rows, listed), jnp.float32),
             pltpu.VMEM((n * q, listed), jnp.float32),
             pltpu.VMEM((n * q, 128), jnp.float32),
-            field, field, field, field, field, field,
-            pltpu.VMEM((GATHERS, n, tall, 128), jnp.float32),
-            pltpu.VMEM((GATHERS, tall, 128), jnp.float32),
-            pltpu.VMEM((GATHERS, tall, 128), jnp.float32),
+            field, field, field, field,
+            pltpu.VMEM((1 + NEWTON, n, q, 128), jnp.float32),
+            pltpu.VMEM((NEWTON, n, tall, 128), jnp.float32),
+            pltpu.VMEM((GATHERS, q, 128), jnp.float32),
+            pltpu.VMEM((GATHERS, q, 128), jnp.float32),
             pltpu.VMEM((n, 8, slots), jnp.float32),
             pltpu.VMEM((n, 8, slots), jnp.float32),
-            pltpu.VMEM((NEWTON, n, 8, 128), jnp.float32),
-            sems(GATHERS), sems(GATHERS), sems(GATHERS), sems(GATHERS),
+            pltpu.VMEM((NEWTON, n, 4, 128), jnp.float32),
+            sems(9), sems(GATHERS), sems(GATHERS), sems(GATHERS), sems(GATHERS),
             sems(1), sems(1), sems(NEWTON), sems(NEWTON),
         ],
         compiler_params=pltpu.CompilerParams(
-            collective_id=0, has_side_effects=True, vmem_limit_bytes=48 * 2**20
+            collective_id=0, has_side_effects=True, vmem_limit_bytes=64 * 2**20
         ),
-    )(
-        heat, start, shift, across(slave), across(master), across(d_weight), across(m_weight),
-        across(gap_cond), across(active),
-    )
+    )(*operands)
 
 
 def solution(mesh):

time: 53.2 us -> 46.8 us (0.88)
  local copies, waits for them, and re-layouts: 8.14 us -> 2.72 us
  Pallas kernels: 44 us -> 43.2 us
    unnamed x20 -> x4, local copies, waits for them, and re-layouts: 8.14 us -> 2.72 us
    pallas_call x1, Pallas kernels: 44 us -> 43.2 us  [on_device(): pl.pallas_call(functools.partial(kernel, n), out_shape=(jax.ShapeDtypeStr...]
where the time goes in v3:
time: 46.8 us; the launch traced here: 46.6 us
  Pallas kernels  43.2 us (92%)
  local copies, waits for them, and re-layouts  2.72 us (6%)
  between operations  0.65 us (1%)
    pallas_call x1, Pallas kernels, on_device(): pl.pallas_call(functools.partial(kernel, n), out_shape=(jax.ShapeDtypeStr...  43.2 us
    unnamed x4, local copies, waits for them, and re-layouts  2.72 us

profile of v3, /device:TPU:0, one launch (start us, length us, event | category | flops | bytes accessed | tf_op | source)
XLA Modules:
  0.0 46.6 jit_solution(13581654556008279294)
XLA Ops:
  0.6 43.2 %shard_map.104 = (f32[256,512]{1,0:T(8,128)}, f32[256,512]{1,0:T(8,128)}) custom-call(f32[256,512]{1,0:T(8,128)} %heat_in.1, f32[256,512]{1,0:T(8,128)} %start_in.1, f32[256,512]{1,0:T(8,128)} %shift_in.1, s32[1,1024]{1,0:T(1,128)} %bitcast.6, s32[1,1024]{1,0:T(1,128)} %bitcast.7, f32[1,1024]{1,0:T(1,128)} %bitcast.8, f32[1,1024]{1,0:T(1,128)} %bitcast.9, ...), custom_call_target="tpu_custom_call" | custom-call | tf_op jit(solution)/shard_map/pallas_call | solution.py:364
  43.8 0.0 copy-start
  43.9 1.9 %copy.13 = f32[256,512]{1,0:T(8,128)} copy(f32[256,512]{1,0:T(8,128)} %get-tuple-element.4) | data formatting | bytes 1048576
  45.8 0.0 copy-done
  45.8 0.8 %copy.14 = f32[256,512]{1,0:T(8,128)} copy(f32[256,512]{1,0:T(8,128)S(1)} %copy-done) | data formatting | bytes 1048576
Async XLA Ops:
  43.8 1.9 %copy-start = (f32[256,512]{1,0:T(8,128)S(1)}, f32[256,512]{1,0:T(8,128)}, u32[]{:S(2)}) copy-start(f32[256,512]{1,0:T(8,128)} %get-tuple-element.5) | copy-start | bytes 1572868

commit v4 on v3

--- a/solution.py
+++ b/solution.py
@@ -113,7 +113,9 @@
 
     def send_all(source, target, send_sem, recv_sem):
         def send(j, carry):
-            to = lax.rem(me + j, n)
+            down = jnp.where(n - j > me, n - j, n - j - 1)
+            up = jnp.where(j - 1 < me, j - 1, j)
+            to = jnp.where(me < n // 2, down, up)
             pltpu.make_async_remote_copy(
                 src_ref=source(to), dst_ref=target, send_sem=send_sem, recv_sem=recv_sem,
                 device_id=(group, to), device_id_type=MESH,
@@ -186,27 +188,31 @@
             (hot_own, own, pick_own, field_of(1)), (hot_other, other, pick_other, field_of(2))
         ):
             low, high = jnp.bitwise_and(face, 127), jnp.right_shift(face, 7)
-            hot[...] = jnp.where(node == low, 1.0, 0.0).astype(jnp.bfloat16)
+            nodes = jnp.where(node == low, 1.0, 0.0).astype(jnp.bfloat16)
+            for k in range(PARTS):
+                hot[k * 128:(k + 1) * 128] = nodes
             block = lax.broadcasted_iota(jnp.int32, pick.shape, 0)
             pick[...] = jnp.where(block == high, weight, 0.0)
         return field_of(3)
 
     def ends(rows_of, hot, pick):
+        rows_here = rows_of.shape[0]
         parts = split(rows_of, PARTS)
+        parts = jnp.concatenate(
+            [parts[k * rows_here:(k + 1) * rows_here] for k in range(PARTS)], axis=1
+        )
         pieces = []
         step = min(listed, 2048)
         for k in range(0, listed, step):
             here = pl.ds(k, step)
-            values = joined(
-                jnp.dot(parts, hot[:, here], preferred_element_type=jnp.float32), PARTS
-            )
+            values = jnp.dot(parts, hot[:, here], preferred_element_type=jnp.float32)
             pieces.append(jnp.sum(values * pick[:, here], axis=0, keepdims=True))
         return jnp.concatenate(pieces, axis=1)
 
     def lift_of(flux):
         total = joined(
             lax.dot_general(
-                split(pick_own[...] * flux, PARTS), hot_own[...], (((1,), (1,)), ((), ())),
+                split(pick_own[...] * flux, PARTS), hot_own[0:128], (((1,), (1,)), ((), ())),
                 preferred_element_type=jnp.float32,
             ),
             PARTS,
@@ -352,7 +358,7 @@
     slots = pairs // 8
     listed = 2 * n * slots
     tall = (q + 2 + 7) // 8 * 8
-    own_rows = (q + 7) // 8 * 8
+    own_rows = (q + 15) // 16 * 16
     field = pltpu.VMEM((rows, width), jnp.float32)
     whole = lambda x: pltpu.VMEM(x.shape, x.dtype)
     sems = lambda count: pltpu.SemaphoreType.DMA((count,))
@@ -367,8 +373,8 @@
         in_specs=[hbm] * 9,
         out_specs=(vmem, vmem),
         scratch_shapes=[whole(x) for x in operands] + [
-            pltpu.VMEM((128, listed), jnp.bfloat16),
-            pltpu.VMEM((128, listed), jnp.bfloat16),
+            pltpu.VMEM((PARTS * 128, listed), jnp.bfloat16),
+            pltpu.VMEM((PARTS * 128, listed), jnp.bfloat16),
             pltpu.VMEM((own_rows, listed), jnp.float32),
             pltpu.VMEM((n * q, listed), jnp.float32),
             pltpu.VMEM((n * q, 128), jnp.float32),

time: 46.8 us -> 46.3 us (0.989)
  no operation moved by 1% of the time
where the time goes in v4:
time: 46.3 us; the launch traced here: 46.1 us
  Pallas kernels  42.8 us (92%)
  local copies, waits for them, and re-layouts  2.72 us (6%)
  between operations  0.65 us (1%)
    pallas_call x1, Pallas kernels, on_device(): pl.pallas_call(functools.partial(kernel, n), out_shape=(jax.ShapeDtypeStr...  42.8 us
    unnamed x4, local copies, waits for them, and re-layouts  2.72 us

profile of v4, /device:TPU:0, one launch (start us, length us, event | category | flops | bytes accessed | tf_op | source)
XLA Modules:
  0.0 46.1 jit_solution(14676388498272251856)
XLA Ops:
  0.6 42.8 %shard_map.104 = (f32[256,512]{1,0:T(8,128)}, f32[256,512]{1,0:T(8,128)}) custom-call(f32[256,512]{1,0:T(8,128)} %heat_in.1, f32[256,512]{1,0:T(8,128)} %start_in.1, f32[256,512]{1,0:T(8,128)} %shift_in.1, s32[1,1024]{1,0:T(1,128)} %bitcast.6, s32[1,1024]{1,0:T(1,128)} %bitcast.7, f32[1,1024]{1,0:T(1,128)} %bitcast.8, f32[1,1024]{1,0:T(1,128)} %bitcast.9, ...), custom_call_target="tpu_custom_call" | custom-call | tf_op jit(solution)/shard_map/pallas_call | solution.py:370
  43.4 0.0 copy-start
  43.4 1.9 %copy.13 = f32[256,512]{1,0:T(8,128)} copy(f32[256,512]{1,0:T(8,128)} %get-tuple-element.4) | data formatting | bytes 1048576
  45.3 0.0 copy-done
  45.4 0.8 %copy.14 = f32[256,512]{1,0:T(8,128)} copy(f32[256,512]{1,0:T(8,128)S(1)} %copy-done) | data formatting | bytes 1048576
Async XLA Ops:
  43.4 1.9 %copy-start = (f32[256,512]{1,0:T(8,128)S(1)}, f32[256,512]{1,0:T(8,128)}, u32[]{:S(2)}) copy-start(f32[256,512]{1,0:T(8,128)} %get-tuple-element.5) | copy-start | bytes 1572868

commit v5 on v4

--- a/solution.py
+++ b/solution.py
@@ -76,11 +76,11 @@
 
 def kernel(
     n, heat_in, start_in, shift_in, slave_in, master_in, d_in, m_in, cond_in, active_in,
-    temp_ref, final_ref,
-    heat_ref, start_ref, shift_ref, slave_ref, master_ref, d_ref, m_ref, cond_ref, active_ref,
+    temp_out, final_out,
+    temp_ref, final_ref, heat_ref, start_ref, shift_ref, slave_ref, master_ref, d_ref, m_ref, cond_ref, active_ref,
     hot_own, hot_other, pick_own, pick_other, faces, kt, r0, w0, kw0,
     plain_buf, sums_buf, hsend_buf, hrecv_buf, rsend_buf, rrecv_buf, fbuf,
-    loads, gsend, grecv, hsend, hrecv, rsend, rrecv, fsend, frecv,
+    loads, stores, gsend, grecv, hsend, hrecv, rsend, rrecv, fsend, frecv,
 ):
     inputs = [
         pltpu.make_async_copy(source, target, loads.at[k])
@@ -339,8 +339,14 @@
         bottom = -(kt[last_row] + (step_0 * w0[last_row] + step_w * kw0[last_row]))
 
     temp_ref[...] = temp_ref[...] + (step_0 * r0[...] + step_w * w0[...])
+    outputs = [
+        pltpu.make_async_copy(temp_ref, temp_out, stores.at[0]),
+        pltpu.make_async_copy(final_ref, final_out, stores.at[1]),
+    ]
+    outputs[0].start()
     final_ref[...] = kt[...] + (step_0 * w0[...] + step_w * kw0[...])
     final_ref[first_row] = lift_of(live * (2.0 * gap_t - arctan(gap_t))) - top
+    outputs[1].start()
 
     for k in range(GATHERS):
         wait_all(slab(k), gsend.at[k])
@@ -348,6 +354,28 @@
     wait_all(rsend_buf, rsend.at[0])
     for k in range(NEWTON):
         wait_all(fbuf.at[k], fsend.at[k])
+    for copy in outputs:
+        copy.wait()
+
+
+def settle(first_in, second_in, first_out, second_out, hold, loads, stores):
+    count, height = hold.shape[0] // 2, hold.shape[1]
+    moves = []
+    for k in range(2 * count):
+        source = (first_in, second_in)[k // count]
+        target = (first_out, second_out)[k // count]
+        here = pl.ds(k % count * height, height)
+        moves.append((
+            pltpu.make_async_copy(source.at[here], hold.at[k], loads.at[k]),
+            pltpu.make_async_copy(hold.at[k], target.at[here], stores.at[k]),
+        ))
+    for load, _ in moves:
+        load.start()
+    for load, store in moves:
+        load.wait()
+        store.start()
+    for _, store in moves:
+        store.wait()
 
 
 def on_device(heat, start, shift, slave, master, d_weight, m_weight, gap_cond, active):
@@ -362,17 +390,16 @@
     field = pltpu.VMEM((rows, width), jnp.float32)
     whole = lambda x: pltpu.VMEM(x.shape, x.dtype)
     sems = lambda count: pltpu.SemaphoreType.DMA((count,))
-    vmem = pl.BlockSpec(memory_space=pltpu.VMEM)
     hbm = pl.BlockSpec(memory_space=pltpu.HBM)
     operands = (heat, start, shift) + tuple(
         x.reshape(1, pairs) for x in (slave, master, d_weight, m_weight, gap_cond, active)
     )
-    return pl.pallas_call(
+    results = pl.pallas_call(
         functools.partial(kernel, n),
         out_shape=(jax.ShapeDtypeStruct((rows, width), jnp.float32),) * 2,
         in_specs=[hbm] * 9,
-        out_specs=(vmem, vmem),
-        scratch_shapes=[whole(x) for x in operands] + [
+        out_specs=(hbm, hbm),
+        scratch_shapes=[field, field] + [whole(x) for x in operands] + [
             pltpu.VMEM((PARTS * 128, listed), jnp.bfloat16),
             pltpu.VMEM((PARTS * 128, listed), jnp.bfloat16),
             pltpu.VMEM((own_rows, listed), jnp.float32),
@@ -386,13 +413,25 @@
             pltpu.VMEM((n, 8, slots), jnp.float32),
             pltpu.VMEM((n, 8, slots), jnp.float32),
             pltpu.VMEM((NEWTON, n, 4, 128), jnp.float32),
-            sems(9), sems(GATHERS), sems(GATHERS), sems(GATHERS), sems(GATHERS),
+            sems(9), sems(2), sems(GATHERS), sems(GATHERS), sems(GATHERS), sems(GATHERS),
             sems(1), sems(1), sems(NEWTON), sems(NEWTON),
         ],
         compiler_params=pltpu.CompilerParams(
             collective_id=0, has_side_effects=True, vmem_limit_bytes=64 * 2**20
         ),
     )(*operands)
+    pieces = 4
+    return pl.pallas_call(
+        settle,
+        out_shape=(jax.ShapeDtypeStruct((rows, width), jnp.float32),) * 2,
+        in_specs=[hbm] * 2,
+        out_specs=(hbm, hbm),
+        scratch_shapes=[
+            pltpu.VMEM((2 * pieces, rows // pieces, width), jnp.float32),
+            sems(2 * pieces), sems(2 * pieces),
+        ],
+        compiler_params=pltpu.CompilerParams(vmem_limit_bytes=64 * 2**20),
+    )(*results)
 
 
 def solution(mesh):

time: 46.3 us -> 45.4 us (0.981)
  local copies, waits for them, and re-layouts: 2.72 us -> 0 us
  Pallas kernels: 42.8 us -> 44.6 us
    unnamed x4 -> x0, local copies, waits for them, and re-layouts: 2.72 us -> none
    pallas_call x0 -> x1, Pallas kernels: none -> 2.09 us  [on_device(): pl.pallas_call(settle, out_shape=(jax.ShapeDtypeStruct((rows, width), jnp...]
where the time goes in v5:
time: 45.4 us; the launch traced here: 45.2 us
  Pallas kernels  44.6 us (98%)
  between operations  0.64 us (1%)
    pallas_call x1, Pallas kernels, on_device(): pl.pallas_call(functools.partial(kernel, n), out_shape=(jax.ShapeDtypeStr...  42.5 us
    pallas_call x1, Pallas kernels, on_device(): pl.pallas_call(settle, out_shape=(jax.ShapeDtypeStruct((rows, width), jnp...  2.09 us

profile of v5, /device:TPU:0, one launch (start us, length us, event | category | flops | bytes accessed | tf_op | source)
XLA Modules:
  0.0 45.2 jit_solution(18121867921531758548)
XLA Ops:
  0.6 42.5 %shard_map.104 = (f32[256,512]{1,0:T(8,128)}, f32[256,512]{1,0:T(8,128)}) custom-call(f32[256,512]{1,0:T(8,128)} %heat_in.1, f32[256,512]{1,0:T(8,128)} %start_in.1, f32[256,512]{1,0:T(8,128)} %shift_in.1, s32[1,1024]{1,0:T(1,128)} %bitcast.6, s32[1,1024]{1,0:T(1,128)} %bitcast.7, f32[1,1024]{1,0:T(1,128)} %bitcast.8, f32[1,1024]{1,0:T(1,128)} %bitcast.9, ...), custom_call_target="tpu_custom_call" | custom-call | tf_op jit(solution)/shard_map/pallas_call | solution.py:397
  43.1 2.1 %shard_map.105 = (f32[256,512]{1,0:T(8,128)}, f32[256,512]{1,0:T(8,128)}) custom-call(f32[256,512]{1,0:T(8,128)} %get-tuple-element.4.first_in, f32[256,512]{1,0:T(8,128)} %get-tuple-element.5.second_in), custom_call_target="tpu_custom_call" | custom-call | tf_op jit(solution)/shard_map/pallas_call | solution.py:424

commit v6 on v5

--- a/solution.py
+++ b/solution.py
@@ -78,7 +78,7 @@
     n, heat_in, start_in, shift_in, slave_in, master_in, d_in, m_in, cond_in, active_in,
     temp_out, final_out,
     temp_ref, final_ref, heat_ref, start_ref, shift_ref, slave_ref, master_ref, d_ref, m_ref, cond_ref, active_ref,
-    hot_own, hot_other, pick_own, pick_other, faces, kt, r0, w0, kw0,
+    hot_own, hot_other, hot_back, pick_own, pick_other, faces, kt, r0, w0, kw0,
     plain_buf, sums_buf, hsend_buf, hrecv_buf, rsend_buf, rrecv_buf, fbuf,
     loads, stores, gsend, grecv, hsend, hrecv, rsend, rrecv, fsend, frecv,
 ):
@@ -96,6 +96,7 @@
     pairs = slave_ref.shape[1]
     q = width // 128
     slots = rsend_buf.shape[2]
+    lifted = (q + 7) // 8 * 8
     listed = hot_own.shape[1]
     me = lax.axis_index("sub")
     group = lax.axis_index("groups")
@@ -193,6 +194,7 @@
                 hot[k * 128:(k + 1) * 128] = nodes
             block = lax.broadcasted_iota(jnp.int32, pick.shape, 0)
             pick[...] = jnp.where(block == high, weight, 0.0)
+        hot_back[...] = hot_own[0:128].T
         return field_of(3)
 
     def ends(rows_of, hot, pick):
@@ -211,8 +213,8 @@
 
     def lift_of(flux):
         total = joined(
-            lax.dot_general(
-                split(pick_own[...] * flux, PARTS), hot_own[0:128], (((1,), (1,)), ((), ())),
+            jnp.dot(
+                split(pick_own[0:lifted] * flux, PARTS), hot_back[...],
                 preferred_element_type=jnp.float32,
             ),
             PARTS,
@@ -402,6 +404,7 @@
         scratch_shapes=[field, field] + [whole(x) for x in operands] + [
             pltpu.VMEM((PARTS * 128, listed), jnp.bfloat16),
             pltpu.VMEM((PARTS * 128, listed), jnp.bfloat16),
+            pltpu.VMEM((listed, 128), jnp.bfloat16),
             pltpu.VMEM((own_rows, listed), jnp.float32),
             pltpu.VMEM((n * q, listed), jnp.float32),
             pltpu.VMEM((n * q, 128), jnp.float32),

time: 45.4 us -> 43.2 us (0.952)
  Pallas kernels: 44.6 us -> 42.4 us
    pallas_call x1, Pallas kernels: 42.5 us -> 40.3 us  [on_device(): pl.pallas_call(functools.partial(kernel, n), out_shape=(jax.ShapeDtypeStr...]
where the time goes in v6:
time: 43.2 us; the launch traced here: 43 us
  Pallas kernels  42.4 us (98%)
  between operations  0.64 us (1%)
    pallas_call x1, Pallas kernels, on_device(): pl.pallas_call(functools.partial(kernel, n), out_shape=(jax.ShapeDtypeStr...  40.3 us
    pallas_call x1, Pallas kernels, on_device(): pl.pallas_call(settle, out_shape=(jax.ShapeDtypeStruct((rows, width), jnp...  2.09 us

profile of v6, /device:TPU:0, one launch (start us, length us, event | category | flops | bytes accessed | tf_op | source)
XLA Modules:
  0.0 43.0 jit_solution(1085613023844626226)
XLA Ops:
  0.6 40.3 %shard_map.104 = (f32[256,512]{1,0:T(8,128)}, f32[256,512]{1,0:T(8,128)}) custom-call(f32[256,512]{1,0:T(8,128)} %heat_in.1, f32[256,512]{1,0:T(8,128)} %start_in.1, f32[256,512]{1,0:T(8,128)} %shift_in.1, s32[1,1024]{1,0:T(1,128)} %bitcast.6, s32[1,1024]{1,0:T(1,128)} %bitcast.7, f32[1,1024]{1,0:T(1,128)} %bitcast.8, f32[1,1024]{1,0:T(1,128)} %bitcast.9, ...), custom_call_target="tpu_custom_call" | custom-call | tf_op jit(solution)/shard_map/pallas_call | solution.py:399
  40.9 2.1 %shard_map.105 = (f32[256,512]{1,0:T(8,128)}, f32[256,512]{1,0:T(8,128)}) custom-call(f32[256,512]{1,0:T(8,128)} %get-tuple-element.4.first_in, f32[256,512]{1,0:T(8,128)} %get-tuple-element.5.second_in), custom_call_target="tpu_custom_call" | custom-call | tf_op jit(solution)/shard_map/pallas_call | solution.py:427
